TPU v7x, 256 devices: a whole 4x4x8 slice. The times are simulated.
256 devices in a mesh: grp: 4 (over z_hi, core), tile: 64 (over y, x, z_lo).
Axes of the slice: x: 4, y: 4, z: 8 (z_hi: 2, z_lo: 4; z = z_hi * 4 + z_lo), core: 2. Of those that a mesh axis runs over, the one named last changes fastest.
Arguments:
- fields: float32 [4, 4, 4096, 1024], P('grp', None, 'tile'), may hold values from -6 to 6
- face_aux: float32 [4, 2, 8, 4096], P('grp', None, None, 'tile'), may hold values from -6 to 6
- block_owner: int32 [4, 32768], P('grp', 'tile'), may hold values from -1 to 32767, as said below
Outputs:
- fields_out: float32 [4, 4, 4096, 1024], P('grp', None, 'tile')
- face_aux_out: float32 [4, 2, 8, 4096], P('grp', None, None, 'tile')
Inputs may be any that keep to these rules, and one draw needn't show every extreme that they name: `block_owner`: the last group's entries are -1. Each LES device's blocks name at most 12 blocks of any one acoustic tile, and exactly 12 of one of them; several LES blocks may name the same acoustic block.
All inputs are finite; a program needn't handle non-finite values.
Results may differ from a plain program's by a relative error of at most 0.0008.
Values may be sent and summed in bfloat16 or wider, within the bound.
A program may use at most 64 MiB of HBM per device.

v0:
```python
import math

import jax
import jax.numpy as jnp
from jax import lax
from jax.sharding import PartitionSpec as P

BLK = 128
CAP = 12


LES_DT = 0.1
VISCOSITY = 1.0
ACOUSTIC_DT = 0.2
MACH = 0.3
TANGENT = 1.0


def extended(value, sides, width, wrap):
    for axis, dim in sides:
        size, length = (lax.axis_size(axis), value.shape[dim])
        up = [(i, (i + 1) % size) for i in range(size if wrap else size - 1)]
        down = [(j, i) for i, j in up]
        last = lax.slice_in_dim(value, length - width, length, axis=dim)
        first = lax.slice_in_dim(value, 0, width, axis=dim)
        before = lax.ppermute(last, axis, up)
        after = lax.ppermute(first, axis, down)
        value = jnp.concatenate([before, value, after], axis=dim)
    return value


def hw_tables(order):
    level = jnp.arange(order, dtype=jnp.float32)
    rates = 0.1 * (level + 1.0)
    coupling = jnp.cos(math.pi * (level + 0.5) / (2.0 * order)) ** 2
    return (rates, coupling)


def diff_rows(ext):
    return (ext[:, :-4] - 8.0 * ext[:, 1:-3] + 8.0 * ext[:, 3:-1] - ext[:, 4:]) / 12.0


def diff_depth(arr):
    padded = jnp.pad(arr, ((0, 0), (0, 0), (2, 2)))
    return (
        padded[:, :, :-4] - 8.0 * padded[:, :, 1:-3] + 8.0 * padded[:, :, 3:-1] - padded[:, :, 4:]
    ) / 12.0


def les_substep(ext):
    core = ext[:, 2:-2]
    across = diff_rows(ext * ext[0:1])
    along = diff_depth(core * core[2:3])
    side = jnp.pad(core, ((0, 0), (0, 0), (1, 1)))
    lap = ext[:, 3:-1] + ext[:, 1:-3] + side[:, :, 2:] + side[:, :, :-2] - 4.0 * core
    return core - LES_DT * (across + along) + VISCOSITY * LES_DT * lap


def source_density(state):
    mix = state[0] * state[0] - state[2] * state[2] + state[1] * state[3]
    side = jnp.pad(mix, ((0, 0), (1, 1)))
    return 0.25 * side[:, :-2] + 0.5 * mix + 0.25 * side[:, 2:]


def ghost_diff(column, lower, upper):
    padded = jnp.concatenate([lower, lower, column, upper, upper], axis=1)
    return (padded[:, :-4] - 8.0 * padded[:, 1:-3] + 8.0 * padded[:, 3:-1] - padded[:, 4:]) / 12.0


def acoustic(ext, aux_ext, rates, coupling):
    core = ext[:, 2:-2]
    press, vel_x, vel_z, dens = (core[0], core[1], core[2], core[3])
    out_low = 0.5 * (press[:, 0] - vel_z[:, 0])
    out_high = 0.5 * (press[:, -1] + vel_z[:, -1])
    outgoing = jnp.stack([out_low, out_high])
    aux = aux_ext[:, :, 1:-1]
    earlier = jnp.concatenate([outgoing[:, None], aux[:, :-1]], axis=1)
    second = aux_ext[:, :, 2:] + aux_ext[:, :, :-2] - 2.0 * aux
    aux_new = aux + ACOUSTIC_DT * (
        -rates[None, :, None] * aux + coupling[None, :, None] * (earlier - aux) + TANGENT * second
    )
    incoming = jnp.mean(aux_new, axis=1)
    p_low = (out_low + incoming[0])[:, None]
    p_high = (out_high + incoming[1])[:, None]
    w_low = (incoming[0] - out_low)[:, None]
    w_high = (out_high - incoming[1])[:, None]
    dz_press = ghost_diff(press, p_low, p_high)
    dz_vel = ghost_diff(vel_z, w_low, w_high)
    dx_all = diff_rows(ext)
    spread = dx_all[1] + dz_vel
    new_press = press + ACOUSTIC_DT * (-MACH * dx_all[0] - spread)
    new_vx = vel_x + ACOUSTIC_DT * (-MACH * dx_all[1] - dx_all[0])
    new_vz = vel_z + ACOUSTIC_DT * (-MACH * dx_all[2] - dz_press)
    new_dens = dens + ACOUSTIC_DT * (-MACH * dx_all[3] - spread)
    return (jnp.stack([new_press, new_vx, new_vz, new_dens]), aux_new)


def accumulate(blocks, targets, count):
    index = jnp.where(targets < 0, count, targets).reshape(-1).astype(jnp.int32)
    flat = blocks.reshape(-1, BLK).astype(jnp.float32)
    return jnp.zeros((count + 1, BLK), jnp.float32).at[index].add(flat)[:-1]


def shards(fields, face_aux, block_owner):
    state = fields[0]
    rows = state.shape[1]
    depth = state.shape[2]
    tiles = lax.axis_size("tile")
    groups = lax.axis_size("grp")
    is_les = lax.axis_index("grp") < groups - 1
    count = rows * depth // BLK
    rates, coupling = hw_tables(face_aux.shape[2])

    def blank(wide):
        return jnp.zeros_like(state)

    narrow = extended(state, (("tile", 1),), 2, False)
    first = lax.cond(is_les, les_substep, blank, narrow)
    again = extended(first, (("tile", 1),), 2, False)
    les_state = lax.cond(is_les, les_substep, blank, again)
    aux_ext = extended(face_aux[0], (("tile", 2),), 1, True)

    def skip_acoustic(ext, cycle):
        return (jnp.zeros_like(state), jnp.zeros_like(face_aux[0]))

    def run_acoustic(ext, cycle):
        return acoustic(ext, cycle, rates, coupling)

    partial_state, aux_new = lax.cond(is_les, skip_acoustic, run_acoustic, narrow, aux_ext)
    blocks = source_density(les_state).reshape(count, BLK).astype(jnp.bfloat16)
    owner = block_owner[0]
    live = owner >= 0
    target = jnp.where(live, owner // count, 0)
    hits = ((target[:, None] == jnp.arange(tiles)[None, :]) & live[:, None]).astype(jnp.int32)
    rank = jnp.sum((jnp.cumsum(hits, axis=0) - hits) * hits, axis=1)
    position = jnp.where(live, target * CAP + rank, tiles * CAP)
    packed = (
        jnp.zeros((tiles * CAP + 1, BLK), jnp.bfloat16)
        .at[position]
        .set(blocks)[:-1]
        .reshape(tiles, CAP, BLK)
    )
    slot_ids = (
        jnp.full((tiles * CAP + 1,), -1, jnp.int32)
        .at[position]
        .set(owner % count)[:-1]
        .reshape(tiles, CAP)
    )
    received, received_ids = (
        lax.all_to_all(packed, "tile", split_axis=0, concat_axis=0, tiled=True),
        lax.all_to_all(slot_ids, "tile", split_axis=0, concat_axis=0, tiled=True),
    )
    local_grid = accumulate(received, received_ids, count)
    source = lax.psum(local_grid.astype(jnp.bfloat16), "grp").astype(jnp.float32)
    acoustic_state = partial_state.at[0].add(ACOUSTIC_DT * source.reshape(rows, depth))
    new_state = jnp.where(is_les, les_state, acoustic_state)
    new_aux = jnp.where(is_les, face_aux[0], aux_new)
    return (new_state[None], new_aux[None])


def solution(mesh):
    return jax.shard_map(
        shards,
        mesh=mesh,
        in_specs=(P("grp", None, "tile", None), P("grp", None, None, "tile"), P("grp", "tile")),
        out_specs=(P("grp", None, "tile", None), P("grp", None, None, "tile")),
        check_vma=False,
    )
```

profile of v0, /device:TPU:1, one launch (start us, length us, event | category | flops | bytes accessed | tf_op | source)
XLA Modules:
  0.0 164.8 jit_solution(10985343268088449596)
XLA Ops:
  7.2 0.0 copy-start.8
  7.2 1.9 %copy.35 = f32[1,4,64,1024]{3,1,2,0:T(4,128)S(1)} copy(f32[1,4,64,1024]{3,2,1,0:T(8,128)} %param.11) | data formatting | bytes 2097152 | tf_op args[0]
  9.1 1.3 collective-permute-start.1
  10.4 5.0 %collective-permute-start = (f32[4,2,1024]{2,0,1:T(4,128)S(1)}, f32[4,2,1024]{2,0,1:T(4,128)S(1)}, u32[]{:S(2)}, u32[]{:S(2)}) collective-permute-start(f32[4,2,1024]{2,0,1:T(4,128)S(1)} %get-tuple-element.118), channel_id=1, source_target_pairs={{0,1},{1,2},{2,3},{3,4},{4,5},{5,6},{6,7},{7,8},{8,9},{9,10},{10,1... | collective-permute-start | bytes 98312 | tf_op jit(solution)/shard_map/ppermute | solution.py:26
  15.4 0.0 copy-done.8
  15.5 1.2 reduce-window.6
  16.7 0.2 slice_reduce_fusion
  17.0 0.1 fusion.76
  17.1 0.0 collective-permute-done.1
  17.1 0.0 collective-permute-done
  17.1 1.3 pad_maximum_fusion.7
  18.4 6.8 %conditional.3 = (f32[4,64,1024]{2,1,0:T(8,128)S(1)}) conditional(s32[]{:T(128)} %convert_element_type.36, () %tuple.50, (f32[4,68,1024]{2,0,1:T(4,128)}, f32[4,64,1024]{2,0,1:T(4,128)S(1)}) %tuple.85), branch_computations={%region_0.0_spmd, %region_1.2_spmd} | conditional | flops 5783552 | bytes 19709960 | solution.py:118
  18.4 0.6 copy.21
  19.1 0.6 broadcast_multiply_fusion.1
  19.7 1.9 %copy.20 = f32[4,68,1024]{2,1,0:T(8,128)S(1)} copy(f32[4,68,1024]{2,0,1:T(4,128)} %get-tuple-element.89) | data formatting | bytes 2228224 | tf_op jit(solution)/shard_map
  21.6 1.9 %broadcast_multiply_fusion = f32[4,68,1024]{2,1,0:T(8,128)S(1)} fusion(f32[68,1024]{1,0:T(8,128)S(1)} %slice_bitcast_fusion, f32[4,68,1024]{2,0,1:T(4,128)} %get-tuple-element.89), kind=kLoop, calls=%fused_computation.28 | loop fusion | flops 278528 | bytes 2506752 | tf_op jit(solution)/shard_map/cond/branch_1_fun/mul | solution.py:52
  23.5 1.7 %fusion.6 = f32[4,64,1024]{2,1,0:T(8,128)S(1)} fusion(f32[4,64,1024]{2,1,0:T(8,128)S(1)} %copy.21, f32[4,64,1024]{2,1,0:T(8,128)S(1)} %broadcast_multiply_fusion.1, f32[4,68,1024]{2,1,0:T(8,128)S(1)} %copy.20, f32[4,68,1024]{2,1,0:T(8,128)S(1)} %broadcast_multiply_fusion), kind=kLoop, calls=%fused_computation.15 | loop fusion | flops 5242880 | bytes 9437184 | tf_op jit(solution)/shard_map/cond/branch_1_fun/add | solution.py:56
  25.2 1.3 collective-permute-start.3
  26.5 4.2 %collective-permute-start.2 = (f32[4,2,1024]{2,1,0:T(2,128)S(1)}, f32[4,2,1024]{2,1,0:T(2,128)S(1)}, u32[]{:S(2)}, u32[]{:S(2)}) collective-permute-start(f32[4,2,1024]{2,1,0:T(2,128)S(1)} %get-tuple-element.116), channel_id=1, source_target_pairs={{0,1},{1,2},{2,3},{3,4},{4,5},{5,6},{6,7},{7,8},{8,9},{9,10},{10,1... | collective-permute-start | bytes 98312 | tf_op jit(solution)/shard_map/ppermute | solution.py:26
  30.8 2.4 %scatter_custom_fusion = s32[769]{0:T(1024)S(1)} fusion(s32[512]{0:T(512)S(1)} %bitcast.126, s32[512]{0:T(512)S(1)} %get-tuple-element.122, s32[]{:T(128)} %constant.158.clone.1), kind=kCustom, calls=%fused_computation.186 | custom fusion | bytes 3080 | tf_op jit(solution)/shard_map/scatter | solution.py:146
  33.2 0.7 all_to_all.11
  33.9 20.7 %all-to-all-start = ((s32[64,1,12]{2,1,0:T(1,128)}), s32[64,1,12]{2,1,0:T(1,128)S(1)}, u32[]{:S(2)}, u32[]{:S(2)}) async-start(s32[64,1,12]{2,1,0:T(1,128)} %bitcast.29), calls=%async_computation | async-start | bytes 65536 | tf_op jit(solution)/shard_map/all_to_all | solution.py:151
  54.6 0.0 collective-permute-done.3
  54.6 0.0 collective-permute-done.2
  54.6 0.2 pad_maximum_fusion.6
  54.8 2.3 %conditional.4 = (f32[4,64,1024]{2,1,0:T(8,128)S(1)}) conditional(s32[]{:T(128)} %convert_element_type.36, () %tuple.49, (f32[4,68,1024]{2,1,0:T(8,128)S(1)}, f32[4,64,1024]{2,1,0:T(8,128)S(1)}) %tuple.52), branch_computations={%region_2.3_spmd, %region_3.4_spmd} | conditional | flops 5783552 | bytes 15384584 | solution.py:120
  54.8 0.1 broadcast_multiply_fusion.3
  55.0 0.1 broadcast_multiply_fusion.2
  55.1 1.8 %fusion.21 = f32[4,64,1024]{2,1,0:T(8,128)S(1)} fusion(f32[4,64,1024]{2,1,0:T(8,128)S(1)} %get-tuple-element.69, f32[4,64,1024]{2,1,0:T(8,128)S(1)} %broadcast_multiply_fusion.3, f32[4,68,1024]{2,1,0:T(8,128)S(1)} %broadcast_multiply_fusion.2, f32[4,68,1024]{2,1,0:T(8,128)S(1)} %get-tuple-element.70), kind=kLoop, calls=%fused_computation.44 | loop fusion | flops 5242880 | bytes 9437184 | tf_op jit(solution)/shard_map/cond/branch_1_fun/add | solution.py:56
  57.1 0.0 copy-start.3
  57.1 0.1 fusion.70
  57.2 0.0 copy-start.7
  57.2 0.2 fusion.67
  57.4 0.1 reshape.317
  57.5 1.8 %scatter_custom_fusion.1 = bf16[769,128]{1,0:T(8,128)(2,1)S(1)} fusion(s32[512]{0:T(512)S(1)} %bitcast.127, bf16[512,128]{1,0:T(8,128)(2,1)S(1)} %reshape.317, bf16[]{:T(256)} %constant.168.clone.1), kind=kCustom, calls=%fused_computation.155 | custom fusion | bytes 196866 | tf_op jit(solution)/shard_map/scatter | solution.py:140
  59.3 0.0 copy-done.3
  59.3 0.8 reshape.303
  60.1 3.2 %all-to-all-done = s32[64,1,12]{2,1,0:T(1,128)S(1)} async-done(((s32[64,1,12]{2,1,0:T(1,128)}), s32[64,1,12]{2,1,0:T(1,128)S(1)}, u32[]{:S(2)}, u32[]{:S(2)}) %all-to-all-start) | async-done | bytes 3104 | tf_op jit(solution)/shard_map/all_to_all | solution.py:151
  63.3 6.9 %all-to-all-start.1 = ((bf16[64,12,128]{2,1,0:T(8,128)(2,1)}), bf16[64,12,128]{2,1,0:T(8,128)(2,1)S(1)}, u32[]{:S(2)}, u32[]{:S(2)}) async-start(bf16[64,12,128]{2,1,0:T(8,128)(2,1)} %reshape.303), calls=%async_computation.1 | async-start | bytes 524288 | tf_op jit(solution)/shard_map/all_to_all | solution.py:150
  70.2 0.0 all-reduce.7.cloned.1.call-start
  70.2 0.0 copy-done.7
  70.2 0.1 fusion.97
  70.3 7.4 %collective-permute-start.5 = (f32[2,8,1]{2,1,0:T(8,128)S(1)}, f32[2,8,1]{2,1,0:T(8,128)S(1)}, u32[]{:S(2)}, u32[]{:S(2)}) collective-permute-start(f32[2,8,1]{2,1,0:T(8,128)S(1)} %get-tuple-element.121), channel_id=1, source_target_pairs={{1,0},{2,1},{3,2},{4,3},{5,4},{6,5},{7,6},{8,7},{9,8},{10,9},{11,1... | collective-permute-start | bytes 200 | tf_op jit(solution)/shard_map/ppermute | solution.py:27
  77.7 0.0 collective-permute-start.4
  77.7 0.8 collective-permute-done.5
  78.5 7.7 %collective-permute-done.4 = f32[2,8,1]{2,1,0:T(8,128)S(1)} collective-permute-done((f32[2,8,1]{2,1,0:T(8,128)S(1)}, f32[2,8,1]{2,1,0:T(8,128)S(1)}, u32[]{:S(2)}, u32[]{:S(2)}) %collective-permute-start.4) | collective-permute-done | bytes 96 | tf_op jit(solution)/shard_map/ppermute | solution.py:26
  86.2 0.1 pad_maximum_fusion.8
  86.3 0.6 broadcast.449
  86.8 0.7 reduce.9
  87.5 0.1 all_to_all.13
  87.7 1.1 conditional.5
  87.8 1.1 broadcast.366.clone
  88.8 0.2 copy.26
  89.0 0.0 copy-start.5
  89.0 0.0 all-to-all-done.1
  89.1 0.0 copy-start.4
  89.1 6.1 %scatter_custom_fusion.2 = f32[513,128]{1,0:T(8,128)S(1)} fusion(s32[768]{0:T(1024)S(1)} %fusion.82, f32[768,128]{1,0:T(8,128)S(1)} %reshape.325, f32[]{:T(128)} %constant.157.clone.1), kind=kCustom, calls=%fused_computation.142 | custom fusion | flops 98304 | bytes 262660 | tf_op jit(solution)/shard_map/scatter-add | solution.py:101
  95.2 0.7 slice.577
  95.9 0.0 all-reduce.7.cloned.1.call-update
  95.9 0.6 select_bitcast_fusion.1
  96.5 59.3 %all-reduce.7.cloned.1.call-done = bf16[512,128]{1,0:T(8,128)(2,1)} async-done(((bf16[512,128]{1,0:T(8,128)(2,1)}), bf16[512,128]{1,0:T(8,128)(2,1)}) %all-reduce.7.cloned.1.call-update) | async-done | bytes 131088 | tf_op jit(solution)/shard_map/psum | solution.py:154
  155.8 0.9 convert_multiply_fusion
  156.8 0.0 copy-done.5
  156.9 1.1 select_bitcast_fusion
  (23 shorter events, 0.4 us)
Async XLA Ops:
  7.2 8.2 %copy-start.8 = (s32[1,512]{1,0:T(1,128)S(1)}, s32[1,512]{1,0:T(1,128)}, u32[]{:S(2)}) copy-start(s32[1,512]{1,0:T(1,128)} %param.13) | copy-start | bytes 6148
  9.1 8.0 %collective-permute-start.1 = (f32[4,2,1024]{2,0,1:T(4,128)S(1)}, f32[4,2,1024]{2,0,1:T(4,128)S(1)}, u32[]{:S(2)}, u32[]{:S(2)}) collective-permute-start(f32[4,2,1024]{2,0,1:T(4,128)S(1)} %get-tuple-element.119), channel_id=1, source_target_pairs={{1,0},{2,1},{3,2},{4,3},{5,4},{6,5},{7,6},{8,7},{9,8},{10,9},{11,1... | collective-permute-start | bytes 98312 | tf_op jit(solution)/shard_map/ppermute | solution.py:27
  10.4 6.7 %collective-permute-start = (f32[4,2,1024]{2,0,1:T(4,128)S(1)}, f32[4,2,1024]{2,0,1:T(4,128)S(1)}, u32[]{:S(2)}, u32[]{:S(2)}) collective-permute-start(f32[4,2,1024]{2,0,1:T(4,128)S(1)} %get-tuple-element.118), channel_id=1, source_target_pairs={{0,1},{1,2},{2,3},{3,4},{4,5},{5,6},{6,7},{7,8},{8,9},{9,10},{10,1... | collective-permute-start | bytes 98312 | tf_op jit(solution)/shard_map/ppermute | solution.py:26
  25.2 29.4 %collective-permute-start.3 = (f32[4,2,1024]{2,1,0:T(2,128)S(1)}, f32[4,2,1024]{2,1,0:T(2,128)S(1)}, u32[]{:S(2)}, u32[]{:S(2)}) collective-permute-start(f32[4,2,1024]{2,1,0:T(2,128)S(1)} %get-tuple-element.117), channel_id=1, source_target_pairs={{1,0},{2,1},{3,2},{4,3},{5,4},{6,5},{7,6},{8,7},{9,8},{10,9},{11,1... | collective-permute-start | bytes 98312 | tf_op jit(solution)/shard_map/ppermute | solution.py:27
  26.5 28.1 %collective-permute-start.2 = (f32[4,2,1024]{2,1,0:T(2,128)S(1)}, f32[4,2,1024]{2,1,0:T(2,128)S(1)}, u32[]{:S(2)}, u32[]{:S(2)}) collective-permute-start(f32[4,2,1024]{2,1,0:T(2,128)S(1)} %get-tuple-element.116), channel_id=1, source_target_pairs={{0,1},{1,2},{2,3},{3,4},{4,5},{5,6},{6,7},{7,8},{8,9},{9,10},{10,1... | collective-permute-start | bytes 98312 | tf_op jit(solution)/shard_map/ppermute | solution.py:26
  33.9 29.4 %all-to-all-start = ((s32[64,1,12]{2,1,0:T(1,128)}), s32[64,1,12]{2,1,0:T(1,128)S(1)}, u32[]{:S(2)}, u32[]{:S(2)}) async-start(s32[64,1,12]{2,1,0:T(1,128)} %bitcast.29), calls=%async_computation | async-start | bytes 65536 | tf_op jit(solution)/shard_map/all_to_all | solution.py:151
  57.1 2.2 %copy-start.3 = (f32[4,64,1024]{2,1,0:T(8,128)}, f32[4,64,1024]{2,1,0:T(8,128)S(1)}, u32[]{:S(2)}) copy-start(f32[4,64,1024]{2,1,0:T(8,128)S(1)} %get-tuple-element.131) | copy-start | bytes 3145732
  57.2 13.0 %copy-start.7 = (f32[1,2,8,64]{3,2,1,0:T(8,128)S(1)}, f32[1,2,8,64]{3,2,1,0:T(8,128)}, u32[]{:S(2)}) copy-start(f32[1,2,8,64]{3,2,1,0:T(8,128)} %param.12) | copy-start | bytes 12292
  63.3 25.8 %all-to-all-start.1 = ((bf16[64,12,128]{2,1,0:T(8,128)(2,1)}), bf16[64,12,128]{2,1,0:T(8,128)(2,1)S(1)}, u32[]{:S(2)}, u32[]{:S(2)}) async-start(bf16[64,12,128]{2,1,0:T(8,128)(2,1)} %reshape.303), calls=%async_computation.1 | async-start | bytes 524288 | tf_op jit(solution)/shard_map/all_to_all | solution.py:150
  70.2 85.6 %all-reduce.7.cloned.1.call-start = ((), (), s32[]{:S(2)}) async-start(), calls=%async_computation.2 | async-start | bytes 262144 | tf_op jit(solution)/shard_map/psum | solution.py:154
  70.3 8.2 %collective-permute-start.5 = (f32[2,8,1]{2,1,0:T(8,128)S(1)}, f32[2,8,1]{2,1,0:T(8,128)S(1)}, u32[]{:S(2)}, u32[]{:S(2)}) collective-permute-start(f32[2,8,1]{2,1,0:T(8,128)S(1)} %get-tuple-element.121), channel_id=1, source_target_pairs={{1,0},{2,1},{3,2},{4,3},{5,4},{6,5},{7,6},{8,7},{9,8},{10,9},{11,1... | collective-permute-start | bytes 200 | tf_op jit(solution)/shard_map/ppermute | solution.py:27
  77.7 8.5 %collective-permute-start.4 = (f32[2,8,1]{2,1,0:T(8,128)S(1)}, f32[2,8,1]{2,1,0:T(8,128)S(1)}, u32[]{:S(2)}, u32[]{:S(2)}) collective-permute-start(f32[2,8,1]{2,1,0:T(8,128)S(1)} %get-tuple-element.120), channel_id=1, source_target_pairs={{0,1},{1,2},{2,3},{3,4},{4,5},{5,6},{6,7},{7,8},{8,9},{9,10},{10,1... | collective-permute-start | bytes 200 | tf_op jit(solution)/shard_map/ppermute | solution.py:26
  89.0 67.8 %copy-start.5 = (f32[4,64,1024]{2,1,0:T(8,128)S(1)}, f32[4,64,1024]{2,1,0:T(8,128)}, u32[]{:S(2)}) copy-start(f32[4,64,1024]{2,1,0:T(8,128)} %get-tuple-element.97) | copy-start | bytes 3145732
  89.1 67.8 %copy-start.4 = (f32[4,64,1024]{2,1,0:T(8,128)S(1)}, f32[4,64,1024]{2,1,0:T(8,128)}, u32[]{:S(2)}) copy-start(f32[4,64,1024]{2,1,0:T(8,128)} %copy-done.3) | copy-start | bytes 3145732
Sparse Core Ops, SparseCore 0:
  96.0 59.7 all-reduce.6
where the time goes:
time: 165 us
  waiting for transfers between devices  71 us (43%)
  starting transfers between devices  46.8 us (28%)
  other arithmetic  19 us (12%)
  between operations  14.4 us (9%)
  local copies, waits for them, and re-layouts  13.4 us (8%)
    psum x1, waiting for transfers between devices, shards(): lax.psum(local_grid.astype(jnp.bfloat16), 'grp').astype(jnp.float32)  59.3 us
    all_to_all x1, starting transfers between devices, shards(): lax.all_to_all(slot_ids, 'tile', split_axis=0, concat_axis=0, tiled=True)  20.7 us
    ppermute x3, starting transfers between devices, extended(): after = lax.ppermute(first, axis, down)  9.94 us
    ppermute x3, starting transfers between devices, extended(): before = lax.ppermute(last, axis, up)  9.18 us
    ppermute x3, waiting for transfers between devices, extended(): before = lax.ppermute(last, axis, up)  7.73 us
    all_to_all x1, starting transfers between devices, shards(): lax.all_to_all(packed, 'tile', split_axis=0, concat_axis=0, tiled=True)  6.89 us
    scatter-add x1, other arithmetic, accumulate(): return jnp.zeros((count + 1, BLK), jnp.float32).at[index].add(flat)[:-1]  6.09 us
    another operation x7, local copies, waits for them, and re-layouts  3.85 us
  transfers between devices with their start and end apart: 9, of which 4 were waited for; matrix products, arithmetic and copies ran while one was open for 8% of the time, Pallas kernels for 0%

commit v1 on v0

v1 whole, which is shorter than its diff:
```python
import functools
import math

import jax
import jax.numpy as jnp
from jax import lax
from jax.experimental import pallas as pl
from jax.experimental.pallas import tpu as pltpu
from jax.sharding import PartitionSpec as P

MESH = pl.DeviceIdType.MESH
F32 = jnp.float32
BF16 = jnp.bfloat16

BLK = 128
SLOT = 16
HALO = 4

LES_DT = 0.1
VISCOSITY = 1.0
ACOUSTIC_DT = 0.2
MACH = 0.3
TANGENT = 1.0
NEAR = 8.0 * LES_DT / 12.0
FAR = LES_DT / 12.0
DIFF = VISCOSITY * LES_DT


def iota(shape, dim):
    return lax.broadcasted_iota(jnp.int32, shape, dim)


def exact_dot(a, b, dims):
    return lax.dot_general(
        a, b, (dims, ((), ())), precision=lax.Precision.HIGHEST, preferred_element_type=F32
    )


def roll(x, shift, axis):
    return pltpu.roll(x, shift % x.shape[axis], axis)


def ahead(one, two):
    lane, sub = iota((1, 8, BLK), 2), iota((1, 8, BLK), 1)
    one, two = roll(one, -1, 2), roll(two, -2, 2)
    own = jnp.where(lane < BLK - 1, one, 0.0) + jnp.where(lane < BLK - 2, two, 0.0)
    cross = jnp.where((lane == BLK - 1) & (sub > 0), one, 0.0) + jnp.where(
        (lane >= BLK - 2) & (sub > 0), two, 0.0
    )
    return own + roll(cross, -1, 1)


def behind(one, two):
    lane, sub = iota((1, 8, BLK), 2), iota((1, 8, BLK), 1)
    one, two = roll(one, 1, 2), roll(two, 2, 2)
    own = jnp.where(lane >= 1, one, 0.0) + jnp.where(lane >= 2, two, 0.0)
    cross = jnp.where((lane == 0) & (sub < 7), one, 0.0) + jnp.where(
        (lane < 2) & (sub < 7), two, 0.0
    )
    return own + roll(cross, 1, 1)


def rows_at(ref, part, row, count, span):
    start = pl.multiple_of((part * span + row) * 8, 8)
    return ref[pl.ds(start, count * 8), :].reshape(count, 8, BLK)


def put_rows(ref, part, row, value, span):
    start = pl.multiple_of((part * span + row) * 8, 8)
    ref[pl.ds(start, value.shape[0] * 8), :] = value.reshape(value.shape[0] * 8, BLK)


def les_rows(src, row, count, span):
    u = rows_at(src, 0, row - 2, count + 4, span)
    w = rows_at(src, 2, row, count, span)
    up, down, far = DIFF - NEAR * u[3:-1], DIFF + NEAR * u[1:-3], FAR * u
    right, left, side = DIFF - NEAR * w, DIFF + NEAR * w, FAR * w
    out = []
    for part in range(4):
        q = rows_at(src, part, row - 2, count + 4, span)
        core, bent = q[2:-2], far * q
        across = up * q[3:-1] + down * q[1:-3] + (bent[4:] - bent[:-4])
        edge = side * core
        along = ahead(right * core, edge) + behind(left * core, -edge)
        out.append((1.0 - 4.0 * DIFF) * core + across + along)
    return out


def source_rows(state):
    mix = state[0] * state[0] - state[2] * state[2] + state[1] * state[3]
    none = jnp.zeros_like(mix)
    quarter = 0.25 * mix
    return ahead(quarter, none) + behind(quarter, none) + 0.5 * mix


def slope_rows(q):
    return (q[:-4] - q[4:] + 8.0 * (q[3:-1] - q[1:-3])) * (1.0 / 12.0)


def slope_depth(q):
    near = (8.0 / 12.0) * q
    far = (1.0 / 12.0) * q
    return ahead(near, -far) + behind(-near, far)


def kernel(
    tiles, fields, face_aux, owner, out, aux_out,
    stage, state, middle, final, own, aux, aux_sides, halo_out, halo_in,
    pack, blocks, packed, ids, ids_in, ids_all, received, spread,
    load_sem, small_sem, halo_send, halo_recv, aux_send, aux_recv,
    id_send, id_recv, relay_send, relay_recv, relay_own, slot_send, slot_recv, ready,
):
    rows = stage.shape[1]
    span = rows + 2 * HALO
    group, tile = lax.axis_index("grp"), lax.axis_index("tile")
    last = lax.axis_size("grp") - 1
    after, before = lax.rem(tile + 1, tiles), lax.rem(tile + tiles - 1, tiles)
    is_les = group < last

    edges = (slice(0, 8), slice(rows - 8, rows), slice(8, rows - 8))
    loads = [
        pltpu.make_async_copy(fields.at[0, :, part], stage.at[:, part], load_sem.at[i])
        for i, part in enumerate(edges)
    ]
    own_load = pltpu.make_async_copy(owner, own, small_sem.at[0])
    aux_load = pltpu.make_async_copy(face_aux.at[0], aux, small_sem.at[1])

    barrier = pltpu.get_barrier_semaphore()
    for copy in loads:
        copy.start()
    aux_load.start()

    @pl.when(is_les)
    def _():
        own_load.start()
        for where in (before, after):
            pl.semaphore_signal(barrier, inc=1, device_id={"tile": where}, device_id_type=MESH)
        pl.semaphore_signal(barrier, inc=1, device_id={"grp": last}, device_id_type=MESH)

    @pl.when(group == last)
    def _():
        @pl.loop(1, tiles)
        def _(step):
            pl.semaphore_signal(
                barrier, inc=1, device_id={"tile": lax.rem(tile + step, tiles)}, device_id_type=MESH
            )

    def spread_rows(first, count):
        for part in range(4):
            for lane in range(8):
                start = (part * span + HALO + first) * 8 + lane
                state[pl.ds(start, count, stride=8), :] = stage[
                    part, first : first + count, lane * BLK : (lane + 1) * BLK
                ]

    loads[0].wait()
    loads[1].wait()
    spread_rows(0, 8)
    spread_rows(rows - 8, 8)
    for part in range(4):
        low = rows_at(state, part, HALO, HALO, span)
        high = rows_at(state, part, rows, HALO, span)
        halo_out[0, part * HALO * 8 : (part + 1) * HALO * 8] = low.reshape(-1, BLK).astype(BF16)
        halo_out[1, part * HALO * 8 : (part + 1) * HALO * 8] = high.reshape(-1, BLK).astype(BF16)

    @pl.when(is_les)
    def _():
        pl.semaphore_wait(barrier, 2)

    @pl.when(group == last)
    def _():
        pl.semaphore_wait(barrier, tiles - 1 + last)

    halos = [
        pltpu.make_async_remote_copy(
            halo_out.at[i], halo_in.at[i], halo_send.at[i], halo_recv.at[i],
            device_id={"tile": where}, device_id_type=MESH,
        )
        for i, where in ((0, before), (1, after))
    ]
    for copy in halos:
        copy.start()

    def take_halos():
        for copy in halos:
            copy.wait_recv()
        for part in range(4):
            piece = slice(part * HALO * 8, (part + 1) * HALO * 8)
            upper = jnp.where(tile == tiles - 1, 0.0, halo_in[0, piece].astype(F32))
            lower = jnp.where(tile == 0, 0.0, halo_in[1, piece].astype(F32))
            put_rows(state, part, 0, lower.reshape(HALO, 8, BLK), span)
            put_rows(state, part, rows + HALO, upper.reshape(HALO, 8, BLK), span)

    def send_halos():
        for copy in halos:
            copy.wait_send()

    def write_part(part):
        for lane in range(8):
            out[0, part, :, lane * BLK : (lane + 1) * BLK] = final[
                pl.ds(part * rows * 8 + lane, rows, stride=8), :
            ]

    @pl.when(is_les)
    def _():
        loads[2].wait()
        spread_rows(8, rows - 16)

        own_load.wait()
        count = own.shape[1]
        owned = own[...]
        live = owned >= 0
        target = lax.shift_right_logical(owned, int(math.log2(count)))
        place = jnp.bitwise_and(owned, count - 1)
        hit = (iota((tiles, count), 0) == target) & live
        hits = jnp.where(hit, 1.0, 0.0)
        earlier = jnp.where(iota((count, count), 0) < iota((count, count), 1), 1.0, 0.0)
        ranks = jnp.dot(hits.astype(BF16), earlier.astype(BF16), preferred_element_type=F32)
        rank = jnp.sum(hits * ranks, axis=0, keepdims=True).astype(jnp.int32)
        slot = jnp.where(live, target * SLOT + rank, -1)
        pack[...] = jnp.where(iota((tiles * SLOT, count), 0) == slot, 1.0, 0.0).astype(BF16)
        high = jnp.where(hit, lax.shift_right_logical(place, 4).astype(F32), 0.0)
        low = jnp.where(hit, (jnp.bitwise_and(place, 15) + 1).astype(F32), 0.0)
        column = rank + lax.rem(tile, 8) * SLOT
        chosen = jnp.where(iota((BLK, count), 0) == column, 1.0, 0.0).astype(BF16)
        digits = lax.dot_general(
            jnp.concatenate([high, low], axis=0).astype(BF16), chosen,
            (((1,), (1,)), ((), ())), preferred_element_type=F32,
        )
        ids[...] = (16.0 * digits[:tiles] + digits[tiles:]).reshape(tiles, 1, BLK)

        def first_step(row, size):
            for part, value in enumerate(les_rows(state, row, size, span)):
                put_rows(middle, part, row, value, span)

        def second_step(row, size):
            values = les_rows(middle, row, size, span)
            for part, value in enumerate(values):
                put_rows(final, part, row - HALO, value, rows)
            start = pl.multiple_of((row - HALO) * 8, 32)
            blocks[pl.ds(start, size * 8), :] = source_rows(values).reshape(-1, BLK).astype(BF16)

        @pl.loop(0, (rows - 4) // 4)
        def _(step):
            first_step(6 + step * 4, 4)

        @pl.loop(0, (rows - 8) // 4)
        def _(step):
            second_step(8 + step * 4, 4)

        pl.semaphore_wait(ready, 1)
        id_copy = pltpu.make_async_remote_copy(
            ids, ids_in.at[group], id_send, id_recv.at[group],
            device_id={"grp": last}, device_id_type=MESH,
        )
        id_copy.start()

        take_halos()
        first_step(2, 4)
        first_step(rows + 2, 4)
        for part in range(4):
            low_rows = rows_at(middle, part, 2, 2, span)
            put_rows(middle, part, 2, jnp.where(tile == 0, 0.0, low_rows), span)
            high_rows = rows_at(middle, part, rows + 4, 2, span)
            put_rows(middle, part, rows + 4, jnp.where(tile == tiles - 1, 0.0, high_rows), span)
        second_step(4, 4)
        second_step(rows, 4)

        chosen_blocks = jnp.dot(pack[...], blocks[...], preferred_element_type=F32)
        packed[...] = chosen_blocks.astype(BF16).reshape(tiles, SLOT, BLK)

        @pl.loop(0, tiles)
        def _(step):
            where = lax.rem(tile + step, tiles)
            pltpu.make_async_remote_copy(
                packed.at[where], received.at[group, tile], slot_send, slot_recv.at[group],
                device_id={"grp": last, "tile": where}, device_id_type=MESH,
            ).start()

        for part in range(4):
            write_part(part)
        aux_load.wait()
        aux_out[0] = aux[...]
        send_halos()
        id_copy.wait_send()
        pltpu.make_async_copy(packed, packed, slot_send).wait()

    @pl.when(group == last)
    def _():
        for part in range(3):
            pl.semaphore_signal(ready, inc=1, device_id={"grp": part}, device_id_type=MESH)
        aux_load.wait()
        turns = [
            pltpu.make_async_remote_copy(
                aux, aux_sides.at[i], aux_send.at[i], aux_recv.at[i],
                device_id={"tile": where}, device_id_type=MESH,
            )
            for i, where in ((0, before), (1, after))
        ]
        for copy in turns:
            copy.start()
        loads[2].wait()
        spread_rows(8, rows - 16)
        take_halos()

        dt = ACOUSTIC_DT

        @pl.loop(0, rows // 4)
        def _(step):
            row = HALO + step * 4
            p, u, w, r = (rows_at(state, part, row - 2, 8, span) for part in range(4))
            dp, du, dw, dr = (slope_rows(q) for q in (p, u, w, r))
            p, u, w, r = (q[2:-2] for q in (p, u, w, r))
            div = du + slope_depth(w)
            news = (
                p + dt * (-MACH * dp - div),
                u + dt * (-MACH * du - dp),
                w + dt * (-MACH * dw - slope_depth(p)),
                r + dt * (-MACH * dr - div),
            )
            for part, value in enumerate(news):
                put_rows(final, part, step * 4, value, rows)

        for copy in turns:
            copy.wait_recv()
        order = aux.shape[1]
        level = iota((order, 1), 0).astype(F32)
        rates = 0.1 * (level + 1.0)
        coupling = 0.5 + 0.5 * jnp.cos(math.pi * (level + 0.5) / order)
        here, there = iota((rows, rows), 0), iota((rows, rows), 1)
        bend = jnp.where(here == there, -2.0, 0.0) + jnp.where(
            (here == there + 1) | (here == there - 1), 1.0, 0.0
        )
        from_after = jnp.where((here == 0) & (there == rows - 1), 1.0, 0.0)
        from_before = jnp.where((here == rows - 1) & (there == 0), 1.0, 0.0)
        lane = iota((8, BLK), 1)
        kind = iota((8, BLK), 0)
        fixes = []
        for face in range(2):
            column = slice(0, BLK) if face == 0 else slice(7 * BLK, 8 * BLK)
            press, vel = stage[0, :, column], stage[2, :, column]
            mixed = 0.5 * (press - vel) if face == 0 else 0.5 * (press + vel)
            pick = jnp.where(lane == (0 if face == 0 else BLK - 1), 1.0, 0.0)
            outgoing = exact_dot(pick, mixed, ((1,), (1,)))[0:1]
            old = aux[face]
            second = (
                exact_dot(old, bend, ((1,), (0,)))
                + exact_dot(aux_sides[0, face], from_after, ((1,), (0,)))
                + exact_dot(aux_sides[1, face], from_before, ((1,), (0,)))
            )
            prior = jnp.concatenate([outgoing, old[:-1]], axis=0)
            new = old + dt * (-rates * old + coupling * (prior - old) + TANGENT * second)
            aux_out[0, face] = new
            incoming = jnp.sum(new, axis=0, keepdims=True) * (1.0 / order)
            ghost_p = outgoing + incoming
            ghost_w = incoming - outgoing if face == 0 else outgoing - incoming
            if face == 0:
                shape = jnp.where(lane == 0, -7.0 / 12.0, 0.0) + jnp.where(lane == 1, 1.0 / 12.0, 0.0)
            else:
                shape = jnp.where(lane == BLK - 1, 7.0 / 12.0, 0.0) + jnp.where(
                    lane == BLK - 2, -1.0 / 12.0, 0.0
                )
            shape = jnp.where(kind == 0, -dt * shape, 0.0)
            wide = [jnp.broadcast_to(g, (8, rows)) for g in (ghost_p, ghost_w)]
            fixes.append([exact_dot(g, shape, ((0,), (0,))) for g in wide])

        def fix(part, which):
            for face, column in ((0, slice(0, BLK)), (1, slice(7 * BLK, 8 * BLK))):
                out[0, part, :, column] = out[0, part, :, column] + fixes[face][which]

        for part in range(1, 4):
            write_part(part)
        fix(2, 0)
        fix(3, 1)

        for part in range(3):
            pltpu.make_async_copy(ids_in.at[part], ids_in.at[part], id_recv.at[part]).wait()
        mine = pltpu.make_async_copy(ids_in.at[:, tile], ids_all.at[:, tile], relay_own)
        mine.start()

        @pl.loop(1, tiles)
        def _(step):
            where = lax.rem(tile + step, tiles)
            pltpu.make_async_remote_copy(
                ids_in.at[:, where], ids_all.at[:, tile], relay_send, relay_recv,
                device_id={"tile": where}, device_id_type=MESH,
            ).start()

        mine.wait()
        others = ids_all.at[:, pl.ds(0, tiles - 1)]
        pltpu.make_async_copy(others, others, relay_recv).wait()
        count = spread.shape[0]
        for part in range(3):
            names = ids_all[part].reshape(tiles // 8, 8, BLK)
            names = jnp.sum(names, axis=1).astype(jnp.int32) - 1
            for piece in range(tiles // 8):
                start = (part * (tiles // 8) + piece) * BLK
                match = iota((count, BLK), 0) == names[piece : piece + 1]
                spread[:, start : start + BLK] = jnp.where(match, 1.0, 0.0).astype(BF16)
        pltpu.make_async_copy(others, others, relay_send).wait()
        for copy in turns:
            copy.wait_send()
        send_halos()

        total = jnp.zeros((count, BLK), F32)
        for part in range(3):
            got = received.at[part]
            pltpu.make_async_copy(got, got, slot_recv.at[part]).wait()
            width = tiles * SLOT
            total += jnp.dot(
                spread[:, part * width : (part + 1) * width],
                received[part].reshape(width, BLK), preferred_element_type=F32,
            )
        final[0:count, :] = final[0:count, :] + dt * total
        write_part(0)
        fix(0, 1)


def shards(tiles, fields, face_aux, block_owner):
    _, parts, rows, depth = fields.shape
    order = face_aux.shape[2]
    count = rows * depth // BLK
    span = rows + 2 * HALO
    vmem = pl.BlockSpec(memory_space=pltpu.VMEM)
    anywhere = pl.BlockSpec(memory_space=pl.ANY)
    dma = pltpu.SemaphoreType.DMA
    return pl.pallas_call(
        functools.partial(kernel, tiles),
        out_shape=(
            jax.ShapeDtypeStruct(fields.shape, F32),
            jax.ShapeDtypeStruct(face_aux.shape, F32),
        ),
        in_specs=[anywhere] * 3,
        out_specs=(vmem, vmem),
        scratch_shapes=[
            pltpu.VMEM((parts, rows, depth), F32),
            pltpu.VMEM((parts * span * 8, BLK), F32),
            pltpu.VMEM((parts * span * 8, BLK), F32),
            pltpu.VMEM((parts * rows * 8, BLK), F32),
            pltpu.VMEM((1, count), jnp.int32),
            pltpu.VMEM((2, order, rows), F32),
            pltpu.VMEM((2, 2, order, rows), F32),
            pltpu.VMEM((2, parts * HALO * 8, BLK), BF16),
            pltpu.VMEM((2, parts * HALO * 8, BLK), BF16),
            pltpu.VMEM((tiles * SLOT, count), BF16),
            pltpu.VMEM((count, BLK), BF16),
            pltpu.VMEM((tiles, SLOT, BLK), BF16),
            pltpu.VMEM((tiles, 1, BLK), F32),
            pltpu.VMEM((3, tiles, 1, BLK), F32),
            pltpu.VMEM((3, tiles, 1, BLK), F32),
            pltpu.VMEM((3, tiles, SLOT, BLK), BF16),
            pltpu.VMEM((count, 3 * tiles * SLOT), BF16),
            dma((3,)), dma((2,)), dma((2,)), dma((2,)), dma((2,)), dma((2,)),
            dma, dma((3,)), dma, dma, dma, dma, dma((3,)),
            pltpu.SemaphoreType.REGULAR,
        ],
        compiler_params=pltpu.CompilerParams(
            collective_id=0, has_side_effects=True, vmem_limit_bytes=40 << 20
        ),
    )(fields, face_aux, block_owner)


def solution(mesh):
    return jax.shard_map(
        functools.partial(shards, mesh.shape["tile"]),
        mesh=mesh,
        in_specs=(P("grp", None, "tile", None), P("grp", None, None, "tile"), P("grp", "tile")),
        out_specs=(P("grp", None, "tile", None), P("grp", None, None, "tile")),
        check_vma=False,
    )
```

time: 165 us -> 33.4 us (0.20)
  waiting for transfers between devices: 71 us -> 0 us
  starting transfers between devices: 46.8 us -> 0 us
  Pallas kernels: 0 us -> 28.4 us
  other arithmetic: 19 us -> 0 us
  between operations: 14.4 us -> 0.65 us
  local copies, waits for them, and re-layouts: 13.4 us -> 4.17 us
    psum x1 -> x0, waiting for transfers between devices: 59.3 us -> none  [shards(): lax.psum(local_grid.astype(jnp.bfloat16), 'grp').astype(jnp.float32)]
    pallas_call x0 -> x1, Pallas kernels: none -> 28.4 us  [shards(): pl.pallas_call(functools.partial(kernel, tiles), out_shape=(jax.ShapeDtyp...]
    all_to_all x2 -> x0, starting transfers between devices: 27.6 us -> none  [the longest x1 20.7 us: shards(): lax.all_to_all(slot_ids, 'tile', split_axis=0, concat_axis=0, tiled=True)]
    ppermute x6 -> x0, starting transfers between devices: 19.1 us -> none  [the longest x3 9.94 us: extended(): after = lax.ppermute(first, axis, down)]
    ppermute x6 -> x0, waiting for transfers between devices: 8.53 us -> none  [the longest x3 7.73 us: extended(): before = lax.ppermute(last, axis, up)]
    scatter-add x2 -> x0, other arithmetic: 6.12 us -> none  [the longest x1 6.09 us: accumulate(): return jnp.zeros((count + 1, BLK), jnp.float32).at[index].add(flat)[:-1]]
    scatter x2 -> x0, local copies, waits for them, and re-layouts: 4.25 us -> none  [the longest x1 2.45 us: shards(): slot_ids = jnp.full((tiles * CAP + 1,), -1, jnp.int32).at[position].set(o...]
    another operation x7 -> x0, local copies, waits for them, and re-layouts: 3.85 us -> none
  transfers between devices with their start and end apart: 9 -> 0, of which waited for: 4 -> 0; matrix products, arithmetic and copies ran while one was open for 8% -> 0% of each run, Pallas kernels for 0% -> 0%
where the time goes in v1:
time: 33.4 us; the launch traced here: 33.3 us
  Pallas kernels  28.4 us (85%)
  local copies, waits for them, and re-layouts  4.17 us (12%)
  between operations  0.65 us (2%)
    pallas_call x1, Pallas kernels, shards(): pl.pallas_call(functools.partial(kernel, tiles), out_shape=(jax.ShapeDtyp...  28.4 us
    unnamed x8, local copies, waits for them, and re-layouts  4.17 us

profile of v1, /device:TPU:1, one launch (start us, length us, event | category | flops | bytes accessed | tf_op | source)
XLA Modules:
  0.0 33.3 jit_solution(6150369380433729581)
XLA Ops:
  0.6 0.0 copy-start
  0.6 1.2 %copy-done = f32[1,4,64,1024]{3,2,1,0:T(8,128)S(1)} copy-done((f32[1,4,64,1024]{3,2,1,0:T(8,128)S(1)}, f32[1,4,64,1024]{3,2,1,0:T(8,128)}, u32[]{:S(2)}) %copy-start) | copy-done | bytes 1048600
  1.9 0.0 copy-start.1
  1.9 0.7 %copy-done.1 = f32[1,2,8,64]{3,2,1,0:T(8,128)S(1)} copy-done((f32[1,2,8,64]{3,2,1,0:T(8,128)S(1)}, f32[1,2,8,64]{3,2,1,0:T(8,128)}, u32[]{:S(2)}) %copy-start.1) | copy-done | bytes 4120
  2.6 0.0 copy-start.2
  2.6 0.7 %copy-done.2 = s32[1,512]{1,0:T(1,128)S(1)} copy-done((s32[1,512]{1,0:T(1,128)S(1)}, s32[1,512]{1,0:T(1,128)}, u32[]{:S(2)}) %copy-start.2) | copy-done | bytes 2072
  3.2 28.4 %shard_map.50 = (f32[1,4,64,1024]{3,2,1,0:T(8,128)S(1)}, f32[1,2,8,64]{3,2,1,0:T(8,128)S(1)}) custom-call(f32[1,4,64,1024]{3,2,1,0:T(8,128)S(1)} %copy-done, f32[1,2,8,64]{3,2,1,0:T(8,128)S(1)} %copy-done.1, s32[1,512]{1,0:T(1,128)S(1)} %copy-done.2), custom_call_target="tpu_custom_call" | custom-call | tf_op jit(solution)/shard_map/pallas_call | solution.py:427
  31.7 1.0 %copy.7 = f32[1,4,64,1024]{3,2,1,0:T(8,128)} copy(f32[1,4,64,1024]{3,2,1,0:T(8,128)S(1)} %get-tuple-element.4) | data formatting | bytes 2097152
  32.7 0.6 %copy.8 = f32[1,2,8,64]{3,2,1,0:T(8,128)} copy(f32[1,2,8,64]{3,2,1,0:T(8,128)S(1)} %get-tuple-element.5) | data formatting | bytes 8192
Async XLA Ops:
  0.6 1.2 %copy-start = (f32[1,4,64,1024]{3,2,1,0:T(8,128)S(1)}, f32[1,4,64,1024]{3,2,1,0:T(8,128)}, u32[]{:S(2)}) copy-start(f32[1,4,64,1024]{3,2,1,0:T(8,128)} %fields.1) | copy-start | bytes 3145732
  1.9 0.7 %copy-start.1 = (f32[1,2,8,64]{3,2,1,0:T(8,128)S(1)}, f32[1,2,8,64]{3,2,1,0:T(8,128)}, u32[]{:S(2)}) copy-start(f32[1,2,8,64]{3,2,1,0:T(8,128)} %face_aux.1) | copy-start | bytes 12292
  2.6 0.7 %copy-start.2 = (s32[1,512]{1,0:T(1,128)S(1)}, s32[1,512]{1,0:T(1,128)}, u32[]{:S(2)}) copy-start(s32[1,512]{1,0:T(1,128)} %owner.1) | copy-start | bytes 6148

commit v2 on v1

--- a/solution.py
+++ b/solution.py
@@ -13,7 +13,10 @@
 BF16 = jnp.bfloat16
 
 BLK = 128
-SLOT = 16
+SLOT = 12
+LANES = 16
+CHUNKS = 4
+WAVES = 2
 HALO = 4
 
 LES_DT = 0.1
@@ -217,11 +220,12 @@
         earlier = jnp.where(iota((count, count), 0) < iota((count, count), 1), 1.0, 0.0)
         ranks = jnp.dot(hits.astype(BF16), earlier.astype(BF16), preferred_element_type=F32)
         rank = jnp.sum(hits * ranks, axis=0, keepdims=True).astype(jnp.int32)
-        slot = jnp.where(live, target * SLOT + rank, -1)
+        turn = jnp.bitwise_and(target - tile, tiles - 1)
+        slot = jnp.where(live, turn * SLOT + rank, -1)
         pack[...] = jnp.where(iota((tiles * SLOT, count), 0) == slot, 1.0, 0.0).astype(BF16)
         high = jnp.where(hit, lax.shift_right_logical(place, 4).astype(F32), 0.0)
         low = jnp.where(hit, (jnp.bitwise_and(place, 15) + 1).astype(F32), 0.0)
-        column = rank + lax.rem(tile, 8) * SLOT
+        column = rank + group * LANES
         chosen = jnp.where(iota((BLK, count), 0) == column, 1.0, 0.0).astype(BF16)
         digits = lax.dot_general(
             jnp.concatenate([high, low], axis=0).astype(BF16), chosen,
@@ -266,16 +270,25 @@
         second_step(4, 4)
         second_step(rows, 4)
 
-        chosen_blocks = jnp.dot(pack[...], blocks[...], preferred_element_type=F32)
-        packed[...] = chosen_blocks.astype(BF16).reshape(tiles, SLOT, BLK)
-
-        @pl.loop(0, tiles)
-        def _(step):
-            where = lax.rem(tile + step, tiles)
-            pltpu.make_async_remote_copy(
-                packed.at[where], received.at[group, tile], slot_send, slot_recv.at[group],
-                device_id={"grp": last, "tile": where}, device_id_type=MESH,
-            ).start()
+        turns = tiles // CHUNKS
+        for chunk in range(CHUNKS):
+            first = chunk * turns
+            chosen_blocks = jnp.dot(
+                pack[first * SLOT : (first + turns) * SLOT], blocks[...], preferred_element_type=F32
+            )
+            packed[first : first + turns] = chosen_blocks.astype(BF16).reshape(
+                turns, SLOT // 2, 2, BLK
+            )
+            wave = first * WAVES // tiles
+
+            @pl.loop(first, first + turns)
+            def _(step):
+                pltpu.make_async_remote_copy(
+                    packed.at[step], received.at[group, step], slot_send,
+                    slot_recv.at[group, wave],
+                    device_id={"grp": last, "tile": lax.rem(tile + step, tiles)},
+                    device_id_type=MESH,
+                ).start()
 
         for part in range(4):
             write_part(part)
@@ -375,45 +388,66 @@
 
         for part in range(3):
             pltpu.make_async_copy(ids_in.at[part], ids_in.at[part], id_recv.at[part]).wait()
-        mine = pltpu.make_async_copy(ids_in.at[:, tile], ids_all.at[:, tile], relay_own)
+        ids[...] = ids_in[0] + ids_in[1] + ids_in[2]
+        mine = pltpu.make_async_copy(ids.at[tile], ids_all.at[0], relay_own)
         mine.start()
 
         @pl.loop(1, tiles)
         def _(step):
             where = lax.rem(tile + step, tiles)
             pltpu.make_async_remote_copy(
-                ids_in.at[:, where], ids_all.at[:, tile], relay_send, relay_recv,
+                ids.at[where], ids_all.at[step], relay_send, relay_recv,
                 device_id={"tile": where}, device_id_type=MESH,
             ).start()
 
         mine.wait()
-        others = ids_all.at[:, pl.ds(0, tiles - 1)]
+        others = ids_all.at[pl.ds(1, tiles - 1)]
         pltpu.make_async_copy(others, others, relay_recv).wait()
-        count = spread.shape[0]
+        count, width = spread.shape[1:]
+        listed = ids_all[...].reshape(tiles, BLK)
+        item = iota((1, tiles * SLOT), 1)
+        turn = lax.shift_right_logical(item * 43691, 19)
+        rank = item - turn * SLOT
         for part in range(3):
-            names = ids_all[part].reshape(tiles // 8, 8, BLK)
-            names = jnp.sum(names, axis=1).astype(jnp.int32) - 1
-            for piece in range(tiles // 8):
-                start = (part * (tiles // 8) + piece) * BLK
-                match = iota((count, BLK), 0) == names[piece : piece + 1]
-                spread[:, start : start + BLK] = jnp.where(match, 1.0, 0.0).astype(BF16)
+            column = jnp.where(iota((BLK, tiles * SLOT), 0) == rank + part * LANES, 1.0, 0.0)
+            names = exact_dot(listed, column, ((1,), (0,)))
+            names = jnp.where(iota((tiles, tiles * SLOT), 0) == turn, names, 0.0)
+            names = jnp.sum(names, axis=0, keepdims=True).astype(jnp.int32) - 1
+            for piece in range(tiles * SLOT // BLK):
+                lanes = slice(piece * BLK, (piece + 1) * BLK)
+                match = iota((count, BLK), 0) == names[:, lanes]
+                spread[part, :, lanes] = jnp.where(match, 1.0, 0.0).astype(BF16)
         pltpu.make_async_copy(others, others, relay_send).wait()
         for copy in turns:
             copy.wait_send()
         send_halos()
 
         total = jnp.zeros((count, BLK), F32)
-        for part in range(3):
-            got = received.at[part]
-            pltpu.make_async_copy(got, got, slot_recv.at[part]).wait()
-            width = tiles * SLOT
-            total += jnp.dot(
-                spread[:, part * width : (part + 1) * width],
-                received[part].reshape(width, BLK), preferred_element_type=F32,
-            )
+        size = tiles // WAVES
+        for wave in range(WAVES):
+            for part in range(3):
+                got = received.at[part, wave * size : (wave + 1) * size]
+                pltpu.make_async_copy(got, got, slot_recv.at[part, wave]).wait()
+                lanes = slice(wave * size * SLOT, (wave + 1) * size * SLOT)
+                total += jnp.dot(
+                    spread[part, :, lanes],
+                    received[part, wave * size : (wave + 1) * size].reshape(size * SLOT, BLK),
+                    preferred_element_type=F32,
+                )
         final[0:count, :] = final[0:count, :] + dt * total
         write_part(0)
         fix(0, 1)
+
+
+def store(state, aux, state_out, aux_out, sem):
+    copies = [
+        pltpu.make_async_copy(a, b, sem.at[i])
+        for i, (a, b) in enumerate(((state, state_out), (aux, aux_out)))
+    ]
+    for copy in copies:
+        copy.start()
+    for copy in copies:
+        copy.wait()
 
 
 def shards(tiles, fields, face_aux, block_owner):
@@ -422,14 +456,14 @@
     count = rows * depth // BLK
     span = rows + 2 * HALO
     vmem = pl.BlockSpec(memory_space=pltpu.VMEM)
-    anywhere = pl.BlockSpec(memory_space=pl.ANY)
+    anywhere = pl.BlockSpec(memory_space=pltpu.HBM)
     dma = pltpu.SemaphoreType.DMA
-    return pl.pallas_call(
+    args = [
+        pltpu.with_memory_space_constraint(a, pltpu.HBM) for a in (fields, face_aux, block_owner)
+    ]
+    results = pl.pallas_call(
         functools.partial(kernel, tiles),
-        out_shape=(
-            jax.ShapeDtypeStruct(fields.shape, F32),
-            jax.ShapeDtypeStruct(face_aux.shape, F32),
-        ),
+        out_shape=(pltpu.VMEM(fields.shape, F32), pltpu.VMEM(face_aux.shape, F32)),
         in_specs=[anywhere] * 3,
         out_specs=(vmem, vmem),
         scratch_shapes=[
@@ -444,20 +478,27 @@
             pltpu.VMEM((2, parts * HALO * 8, BLK), BF16),
             pltpu.VMEM((tiles * SLOT, count), BF16),
             pltpu.VMEM((count, BLK), BF16),
-            pltpu.VMEM((tiles, SLOT, BLK), BF16),
+            pltpu.VMEM((tiles, SLOT // 2, 2, BLK), BF16),
             pltpu.VMEM((tiles, 1, BLK), F32),
             pltpu.VMEM((3, tiles, 1, BLK), F32),
-            pltpu.VMEM((3, tiles, 1, BLK), F32),
-            pltpu.VMEM((3, tiles, SLOT, BLK), BF16),
-            pltpu.VMEM((count, 3 * tiles * SLOT), BF16),
+            pltpu.VMEM((tiles, 1, BLK), F32),
+            pltpu.VMEM((3, tiles, SLOT // 2, 2, BLK), BF16),
+            pltpu.VMEM((3, count, tiles * SLOT), BF16),
             dma((3,)), dma((2,)), dma((2,)), dma((2,)), dma((2,)), dma((2,)),
-            dma, dma((3,)), dma, dma, dma, dma, dma((3,)),
+            dma, dma((3,)), dma, dma, dma, dma, dma((3, WAVES)),
             pltpu.SemaphoreType.REGULAR,
         ],
         compiler_params=pltpu.CompilerParams(
             collective_id=0, has_side_effects=True, vmem_limit_bytes=40 << 20
         ),
-    )(fields, face_aux, block_owner)
+    )(*args)
+    return pl.pallas_call(
+        store,
+        out_shape=(pltpu.HBM(fields.shape, F32), pltpu.HBM(face_aux.shape, F32)),
+        in_specs=[vmem, vmem],
+        out_specs=(anywhere, anywhere),
+        scratch_shapes=[dma((2,))],
+    )(*results)
 
 
 def solution(mesh):

time: 33.4 us -> 30.2 us (0.904)
  local copies, waits for them, and re-layouts: 4.17 us -> 1.56 us
  Pallas kernels: 28.4 us -> 27.9 us
    unnamed x8 -> x4, local copies, waits for them, and re-layouts: 4.17 us -> 1.56 us
    pallas_call x1 -> x2, Pallas kernels: 28.4 us -> 27.9 us  [the longest x1 25.7 us: shards(): pl.pallas_call(functools.partial(kernel, tiles), out_shape=(pltpu.VMEM(fi...]
where the time goes in v2:
time: 30.2 us; the launch traced here: 30.1 us
  Pallas kernels  27.9 us (92%)
  local copies, waits for them, and re-layouts  1.56 us (5%)
  between operations  0.65 us (2%)
    pallas_call x1, Pallas kernels, shards(): pl.pallas_call(functools.partial(kernel, tiles), out_shape=(pltpu.VMEM(fi...  25.7 us
    pallas_call x1, Pallas kernels, shards(): pl.pallas_call(store, out_shape=(pltpu.HBM(fields.shape, F32), pltpu.HBM(...  2.21 us
    unnamed x4, local copies, waits for them, and re-layouts  1.56 us

profile of v2, /device:TPU:1, one launch (start us, length us, event | category | flops | bytes accessed | tf_op | source)
XLA Modules:
  0.0 30.1 jit_solution(13862118303746444037)
XLA Ops:
  0.6 25.7 %shard_map.50 = (f32[1,4,64,1024]{3,2,1,0:T(8,128)S(1)}, f32[1,2,8,64]{3,2,1,0:T(8,128)S(1)}) custom-call(f32[1,4,64,1024]{3,2,1,0:T(8,128)} %fields.1, f32[1,2,8,64]{3,2,1,0:T(8,128)} %face_aux.1, s32[1,512]{1,0:T(1,128)} %owner.1), custom_call_target="tpu_custom_call" | custom-call | tf_op jit(solution)/shard_map/pallas_call | solution.py:464
  26.3 0.0 copy-start
  26.3 1.0 %copy-done = f32[1,4,64,1024]{3,2,1,0:T(8,128)} copy-done((f32[1,4,64,1024]{3,2,1,0:T(8,128)}, f32[1,4,64,1024]{3,2,1,0:T(8,128)S(1)}, u32[]{:S(2)}) %copy-start) | copy-done | bytes 1048600
  27.3 0.0 copy-start.1
  27.3 0.6 %copy-done.1 = f32[1,2,8,64]{3,2,1,0:T(8,128)} copy-done((f32[1,2,8,64]{3,2,1,0:T(8,128)}, f32[1,2,8,64]{3,2,1,0:T(8,128)S(1)}, u32[]{:S(2)}) %copy-start.1) | copy-done | bytes 4120
  27.9 2.2 %shard_map.51 = (f32[1,4,64,1024]{3,2,1,0:T(8,128)}, f32[1,2,8,64]{3,2,1,0:T(8,128)}) custom-call(f32[1,4,64,1024]{3,2,1,0:T(8,128)} %copy-done, f32[1,2,8,64]{3,2,1,0:T(8,128)} %copy-done.1), custom_call_target="tpu_custom_call" | custom-call | tf_op jit(solution)/shard_map/pallas_call | solution.py:495
Async XLA Ops:
  26.3 1.0 %copy-start = (f32[1,4,64,1024]{3,2,1,0:T(8,128)}, f32[1,4,64,1024]{3,2,1,0:T(8,128)S(1)}, u32[]{:S(2)}) copy-start(f32[1,4,64,1024]{3,2,1,0:T(8,128)S(1)} %get-tuple-element.4.state) | copy-start | bytes 3145732
  27.3 0.6 %copy-start.1 = (f32[1,2,8,64]{3,2,1,0:T(8,128)}, f32[1,2,8,64]{3,2,1,0:T(8,128)S(1)}, u32[]{:S(2)}) copy-start(f32[1,2,8,64]{3,2,1,0:T(8,128)S(1)} %get-tuple-element.5.aux) | copy-start | bytes 12292

commit v3 on v1

v3 whole, which is shorter than its diff:
```python
import functools
import math

import jax
import jax.numpy as jnp
from jax import lax
from jax.experimental import pallas as pl
from jax.experimental.pallas import tpu as pltpu
from jax.sharding import PartitionSpec as P

MESH = pl.DeviceIdType.MESH


def ring(step):
    return min(step, 4 - step)


F32 = jnp.float32
BF16 = jnp.bfloat16

BLK = 128
SLOT = 12
LANES = 16
COLUMNS = sorted(range(16), key=lambda c: (-ring(c // 4) - ring(c % 4), c))
FAR_COLUMNS = sum(ring(c // 4) + ring(c % 4) > 2 for c in COLUMNS)
HALO = 4

LES_DT = 0.1
VISCOSITY = 1.0
ACOUSTIC_DT = 0.2
MACH = 0.3
TANGENT = 1.0
NEAR = 8.0 * LES_DT / 12.0
FAR = LES_DT / 12.0
DIFF = VISCOSITY * LES_DT


def iota(shape, dim):
    return lax.broadcasted_iota(jnp.int32, shape, dim)


def tile_at(tile, column, step):
    y, x, z = tile // 16, lax.rem(tile // 4, 4), lax.rem(tile, 4)
    y, x = lax.rem(y + column // 4, 4), lax.rem(x + column % 4, 4)
    z = (3 - z, 2 + lax.rem(z, 2) * 2 - z, 1 + z // 2 * 4 - z, z)[step]
    return y * 16 + x * 4 + z


def turn_of(target, tile):
    y, x, z = tile // 16, lax.rem(tile // 4, 4), lax.rem(tile, 4)
    dy = jnp.bitwise_and(lax.shift_right_logical(target, 4) - y, 3)
    dx = jnp.bitwise_and(lax.shift_right_logical(target, 2) - x, 3)
    dz = 3 - jnp.bitwise_xor(jnp.bitwise_and(target, 3), z)
    code = dy * 4 + dx
    place = jnp.zeros_like(code)
    for i, column in enumerate(COLUMNS):
        place = jnp.where(code == column, i, place)
    return place * 4 + dz


def exact_dot(a, b, dims):
    return lax.dot_general(
        a, b, (dims, ((), ())), precision=lax.Precision.HIGHEST, preferred_element_type=F32
    )


def roll(x, shift, axis):
    return pltpu.roll(x, shift % x.shape[axis], axis)


def ahead(one, two):
    lane, sub = iota((1, 8, BLK), 2), iota((1, 8, BLK), 1)
    one, two = roll(one, -1, 2), roll(two, -2, 2)
    own = jnp.where(lane < BLK - 1, one, 0.0) + jnp.where(lane < BLK - 2, two, 0.0)
    cross = jnp.where((lane == BLK - 1) & (sub > 0), one, 0.0) + jnp.where(
        (lane >= BLK - 2) & (sub > 0), two, 0.0
    )
    return own + roll(cross, -1, 1)


def behind(one, two):
    lane, sub = iota((1, 8, BLK), 2), iota((1, 8, BLK), 1)
    one, two = roll(one, 1, 2), roll(two, 2, 2)
    own = jnp.where(lane >= 1, one, 0.0) + jnp.where(lane >= 2, two, 0.0)
    cross = jnp.where((lane == 0) & (sub < 7), one, 0.0) + jnp.where(
        (lane < 2) & (sub < 7), two, 0.0
    )
    return own + roll(cross, 1, 1)


def rows_at(ref, part, row, count, span):
    start = pl.multiple_of((part * span + row) * 8, 8)
    return ref[pl.ds(start, count * 8), :].reshape(count, 8, BLK)


def put_rows(ref, part, row, value, span):
    start = pl.multiple_of((part * span + row) * 8, 8)
    ref[pl.ds(start, value.shape[0] * 8), :] = value.reshape(value.shape[0] * 8, BLK)


def les_rows(src, row, count, span):
    u = rows_at(src, 0, row - 2, count + 4, span)
    w = rows_at(src, 2, row, count, span)
    up, down, far = DIFF - NEAR * u[3:-1], DIFF + NEAR * u[1:-3], FAR * u
    right, left, side = DIFF - NEAR * w, DIFF + NEAR * w, FAR * w
    out = []
    for part in range(4):
        q = rows_at(src, part, row - 2, count + 4, span)
        core, bent = q[2:-2], far * q
        across = up * q[3:-1] + down * q[1:-3] + (bent[4:] - bent[:-4])
        edge = side * core
        along = ahead(right * core, edge) + behind(left * core, -edge)
        out.append((1.0 - 4.0 * DIFF) * core + across + along)
    return out


def source_rows(state):
    mix = state[0] * state[0] - state[2] * state[2] + state[1] * state[3]
    none = jnp.zeros_like(mix)
    quarter = 0.25 * mix
    return ahead(quarter, none) + behind(quarter, none) + 0.5 * mix


def slope_rows(q):
    return (q[:-4] - q[4:] + 8.0 * (q[3:-1] - q[1:-3])) * (1.0 / 12.0)


def slope_depth(q):
    near = (8.0 / 12.0) * q
    far = (1.0 / 12.0) * q
    return ahead(near, -far) + behind(-near, far)


def spread_rows(stage, state, first, count):
    span = state.shape[0] // 32
    for part in range(4):
        for lane in range(8):
            start = (part * span + HALO + first) * 8 + lane
            state[pl.ds(start, count, stride=8), :] = stage[
                part, first : first + count, lane * BLK : (lane + 1) * BLK
            ]


def write_part(final, out, part):
    rows = out.shape[2]
    for lane in range(8):
        out[0, part, :, lane * BLK : (lane + 1) * BLK] = final[
            pl.ds(part * rows * 8 + lane, rows, stride=8), :
        ]


class Halos:
    def __init__(self, tiles, tile, state, halo_out, halo_in, send, recv):
        self.state, self.halo_out, self.halo_in = state, halo_out, halo_in
        self.has_before, self.has_after = tile > 0, tile < tiles - 1
        wheres = (lax.rem(tile + tiles - 1, tiles), lax.rem(tile + 1, tiles))
        self.copies = [
            pltpu.make_async_remote_copy(
                halo_out.at[i], halo_in.at[i], send.at[i], recv.at[i],
                device_id={"tile": where}, device_id_type=MESH,
            )
            for i, where in enumerate(wheres)
        ]
        self.span = state.shape[0] // 32
        self.rows = self.span - 2 * HALO

    def pack(self):
        for part in range(4):
            piece = slice(part * HALO * 8, (part + 1) * HALO * 8)
            low = rows_at(self.state, part, HALO, HALO, self.span)
            high = rows_at(self.state, part, self.rows, HALO, self.span)
            self.halo_out[0, piece] = low.reshape(-1, BLK).astype(BF16)
            self.halo_out[1, piece] = high.reshape(-1, BLK).astype(BF16)

    def start(self):
        for copy, there in zip(self.copies, (self.has_before, self.has_after)):
            pl.when(there)(copy.start)

    def take(self):
        for copy, there in zip(self.copies, (self.has_after, self.has_before)):
            pl.when(there)(copy.wait_recv)
        for part in range(4):
            piece = slice(part * HALO * 8, (part + 1) * HALO * 8)
            upper = jnp.where(self.has_after, self.halo_in[0, piece].astype(F32), 0.0)
            lower = jnp.where(self.has_before, self.halo_in[1, piece].astype(F32), 0.0)
            put_rows(self.state, part, 0, lower.reshape(HALO, 8, BLK), self.span)
            put_rows(self.state, part, self.rows + HALO, upper.reshape(HALO, 8, BLK), self.span)

    def finish(self):
        for copy, there in zip(self.copies, (self.has_before, self.has_after)):
            pl.when(there)(copy.wait_send)


def row_loads(fields, stage, sem):
    rows = stage.shape[1]
    edges = (slice(0, 8), slice(rows - 8, rows), slice(8, rows - 8))
    return [
        pltpu.make_async_copy(fields.at[0, :, part], stage.at[:, part], sem.at[i])
        for i, part in enumerate(edges)
    ]


def les_kernel(
    tiles, fields, owner, final, packed, names,
    stage, state, middle, own, halo_out, halo_in, pack, blocks, ids,
    load_sem, own_sem, halo_send, halo_recv, id_send, id_recv,
):
    rows = stage.shape[1]
    span = rows + 2 * HALO
    group, tile = lax.axis_index("grp"), lax.axis_index("tile")
    last = lax.axis_size("grp") - 1
    halos = Halos(tiles, tile, state, halo_out, halo_in, halo_send, halo_recv)
    barrier = pltpu.get_barrier_semaphore()

    @pl.when(group < last)
    def _():
        loads = row_loads(fields, stage, load_sem)
        own_load = pltpu.make_async_copy(owner, own, own_sem)
        for copy in loads[:2]:
            copy.start()
        own_load.start()
        loads[2].start()

        @pl.when(group < 2)
        def _():
            pl.semaphore_signal(
                barrier, inc=1, device_id={"grp": lax.rem(group + 1, 2)}, device_id_type=MESH
            )

        for there, step in ((halos.has_before, tiles - 1), (halos.has_after, 1)):

            @pl.when(there)
            def _():
                pl.semaphore_signal(
                    barrier, inc=1, device_id={"tile": lax.rem(tile + step, tiles)},
                    device_id_type=MESH,
                )

        loads[0].wait()
        loads[1].wait()
        spread_rows(stage, state, 0, 8)
        spread_rows(stage, state, rows - 8, 8)
        halos.pack()
        paired = group < 2
        neighbours = halos.has_before.astype(jnp.int32) + halos.has_after.astype(jnp.int32)
        neighbours = neighbours + paired.astype(jnp.int32)
        id_copy = pltpu.make_async_remote_copy(
            ids.at[0], ids.at[1], id_send, id_recv,
            device_id={"grp": lax.rem(group + 1, 2)}, device_id_type=MESH,
        )
        chip = lax.rem(tile, 4)

        def meet():
            pl.semaphore_wait(barrier, neighbours)
            halos.start()

        pl.when(chip == 3)(meet)
        own_load.wait()
        count = own.shape[1]
        owned = own[...]
        live = owned >= 0
        target = lax.shift_right_logical(owned, int(math.log2(count)))
        place = jnp.bitwise_and(owned, count - 1)
        turn = turn_of(target, tile)
        hit = (iota((tiles, count), 0) == turn) & live
        hits = jnp.where(hit, 1.0, 0.0)
        earlier = jnp.where(iota((count, count), 0) < iota((count, count), 1), 1.0, 0.0)
        ranks = jnp.dot(hits.astype(BF16), earlier.astype(BF16), preferred_element_type=F32)
        rank = jnp.sum(hits * ranks, axis=0, keepdims=True).astype(jnp.int32)
        slot = jnp.where(live, turn * SLOT + rank, -1)
        pack[...] = jnp.where(iota((tiles * SLOT, count), 0) == slot, 1.0, 0.0).astype(BF16)
        listed = (iota((8, count), 0) == lax.shift_right_logical(turn, 3)) & live
        high = jnp.where(listed, lax.shift_right_logical(place, 4).astype(F32), 0.0)
        low = jnp.where(listed, (jnp.bitwise_and(place, 15) + 1).astype(F32), 0.0)
        lane = jnp.bitwise_and(turn, 7) * LANES + rank
        chosen = jnp.where(iota((BLK, count), 0) == lane, 1.0, 0.0).astype(BF16)
        digits = lax.dot_general(
            jnp.concatenate([high, low], axis=0).astype(BF16), chosen,
            (((1,), (1,)), ((), ())), preferred_element_type=F32,
        )
        ids[0] = 16.0 * digits[:8] + digits[8:]
        loads[2].wait()
        spread_rows(stage, state, 8, rows - 16)

        def first_step(row, size):
            for part, value in enumerate(les_rows(state, row, size, span)):
                put_rows(middle, part, row, value, span)

        def second_step(row, size):
            values = les_rows(middle, row, size, span)
            for part, value in enumerate(values):
                put_rows(final, part, row - HALO, value, rows)
            start = (row - HALO) * 8
            blocks[start : start + size * 8, :] = source_rows(values).reshape(-1, BLK).astype(BF16)

        first_step(6, rows - 4)
        pl.when((chip == 1) | (chip == 2))(meet)
        second_step(8, rows - 8)
        pl.when(chip == 0)(meet)
        pl.when(paired)(id_copy.start)
        pl.when(paired)(id_copy.wait_recv)
        turns, lane = iota((tiles, BLK), 0), iota((tiles, BLK), 1)
        chosen_row = jnp.where(iota((tiles, 8), 1) == iota((tiles, 8), 0) // 8, 1.0, 0.0)
        kept = lax.shift_right_logical(lane, 4) == jnp.bitwise_and(turns, 7)
        folded = jnp.bitwise_and(iota((BLK, BLK), 0), LANES - 1)

        def placed(listed, part):
            listed = jnp.where(kept, exact_dot(chosen_row, listed, ((1,), (0,))), 0.0)
            fold = jnp.where(iota((BLK, BLK), 1) == folded + part * LANES, 1.0, 0.0)
            return exact_dot(listed, fold, ((1,), (0,)))

        others = jnp.where(paired, ids[1], 0.0)
        listed = placed(ids[0], group) + placed(others, lax.rem(group + 1, 2))
        names[...] = listed.reshape(tiles, 1, BLK)

        halos.take()
        tops, bottoms = les_rows(state, 2, 4, span), les_rows(state, rows + 2, 4, span)
        for part in range(4):
            put_rows(middle, part, 2, tops[part], span)
            put_rows(middle, part, rows + 2, bottoms[part], span)
        for part in range(4):
            low_rows = rows_at(middle, part, 2, 2, span)
            put_rows(middle, part, 2, jnp.where(halos.has_before, low_rows, 0.0), span)
            high_rows = rows_at(middle, part, rows + 4, 2, span)
            put_rows(middle, part, rows + 4, jnp.where(halos.has_after, high_rows, 0.0), span)
        tops, bottoms = les_rows(middle, 4, 4, span), les_rows(middle, rows, 4, span)
        for values, row in ((tops, 0), (bottoms, rows - 4)):
            for part in range(4):
                put_rows(final, part, row, values[part], rows)
            start = row * 8
            blocks[start : start + 32, :] = source_rows(values).reshape(-1, BLK).astype(BF16)
        chosen_blocks = jnp.dot(pack[...], blocks[...], preferred_element_type=F32)
        packed[...] = chosen_blocks.astype(BF16).reshape(packed.shape)
        halos.finish()
        pl.when(paired)(id_copy.wait_send)


def exchange_kernel(
    tiles, fields, face_aux, les, packed, names, out, aux_out,
    stage, state, final, aux, aux_sides, halo_out, halo_in,
    names_in, received, spread,
    load_sem, aux_sem, halo_send, halo_recv, aux_send, aux_recv,
    name_send, name_recv, slot_send, slot_recv, partner_in,
):
    rows = stage.shape[1]
    span = rows + 2 * HALO
    group, tile = lax.axis_index("grp"), lax.axis_index("tile")
    last = lax.axis_size("grp") - 1
    after, before = lax.rem(tile + 1, tiles), lax.rem(tile + tiles - 1, tiles)
    halos = Halos(tiles, tile, state, halo_out, halo_in, halo_send, halo_recv)
    barrier = pltpu.get_barrier_semaphore()
    far = 4 * FAR_COLUMNS
    waves = [(0, far), (far, far + 24), (far + 24, tiles - 8), (tiles - 8, tiles)]

    half = tiles // 2

    def send(name_turns, order):
        def send_names(turn, which):
            pltpu.make_async_remote_copy(
                names.at[turn], names_in.at[which, turn], name_send, name_recv.at[which],
                device_id=there(COLUMNS[turn // 4], turn % 4), device_id_type=MESH,
            ).start()

        there = lambda c, k: {"grp": last, "tile": tile_at(tile, c, k)}
        which = 1 if len(name_turns) == tiles else 0
        for turn in name_turns:
            send_names(turn, which)
        for place, column in enumerate(COLUMNS):
            wave = sum(end <= 4 * place for _, end in waves)
            for step in order:
                turn = 4 * place + step
                pltpu.make_async_remote_copy(
                    packed.at[turn], received.at[group, turn], slot_send,
                    slot_recv.at[which, wave], device_id=there(column, step), device_id_type=MESH,
                ).start()

    def tell(sem, **there):
        pl.semaphore_signal(sem, inc=1, device_id=there, device_id_type=MESH)

    for mine, heard in ((0, far), (1, tiles - far)):

        @pl.when(group == mine)
        def _():
            tell(barrier, grp=1 - mine)
            pl.semaphore_wait(barrier, heard + 1)
            tell(partner_in, grp=1 - mine)
            pl.semaphore_wait(partner_in, 1)
            send(range(mine * half, (mine + 1) * half), (3, 2, 1, 0))
            sent = names.at[pl.ds(0, half)]
            pltpu.make_async_copy(sent, sent, name_send).wait()

    @pl.when(group == 2)
    def _():
        pl.semaphore_wait(barrier, tiles)
        send(range(tiles), range(4))
        pltpu.make_async_copy(names, names, name_send).wait()

    @pl.when(group < last)
    def _():
        for part in range(4):
            write_part(les, out, part)
        aux_load = pltpu.make_async_copy(face_aux.at[0], aux_out.at[0], aux_sem)
        aux_load.start()
        aux_load.wait()
        pltpu.make_async_copy(packed, packed, slot_send).wait()

    @pl.when(group == last)
    def _():
        for where in (before, after):
            pl.semaphore_signal(barrier, inc=1, device_id={"tile": where}, device_id_type=MESH)

        for place, column in enumerate(COLUMNS):

            for step in range(4):
                where = tile_at(tile, column, step)
                tell(barrier, grp=0 if place < FAR_COLUMNS else 1, tile=where)
                tell(barrier, grp=2, tile=where)

        loads = row_loads(fields, stage, load_sem)
        aux_load = pltpu.make_async_copy(face_aux.at[0], aux, aux_sem)
        for copy in loads:
            copy.start()
        aux_load.start()
        for copy in loads:
            copy.wait()
        spread_rows(stage, state, 0, rows)
        halos.pack()
        aux_load.wait()
        turns = [
            pltpu.make_async_remote_copy(
                aux, aux_sides.at[i], aux_send.at[i], aux_recv.at[i],
                device_id={"tile": where}, device_id_type=MESH,
            )
            for i, where in ((0, before), (1, after))
        ]
        pl.semaphore_wait(barrier, 2)
        halos.start()
        for copy in turns:
            copy.start()
        halos.take()

        dt = ACOUSTIC_DT

        size = rows // 4

        @pl.loop(0, 4)
        def _(step):
            row = HALO + step * size
            p, u, w, r = (rows_at(state, part, row - 2, size + 4, span) for part in range(4))
            dp, du, dw, dr = (slope_rows(q) for q in (p, u, w, r))
            p, u, w, r = (q[2:-2] for q in (p, u, w, r))
            div = du + slope_depth(w)
            news = (
                p + dt * (-MACH * dp - div),
                u + dt * (-MACH * du - dp),
                w + dt * (-MACH * dw - slope_depth(p)),
                r + dt * (-MACH * dr - div),
            )
            for part, value in enumerate(news):
                put_rows(final, part, step * size, value, rows)

        for copy in turns:
            copy.wait_recv()
        order = aux.shape[1]
        level = iota((order, 1), 0).astype(F32)
        rates = 0.1 * (level + 1.0)
        coupling = 0.5 + 0.5 * jnp.cos(math.pi * (level + 0.5) / order)
        here, there = iota((rows, rows), 0), iota((rows, rows), 1)
        bend = jnp.where(here == there, -2.0, 0.0) + jnp.where(
            (here == there + 1) | (here == there - 1), 1.0, 0.0
        )
        from_after = jnp.where((here == 0) & (there == rows - 1), 1.0, 0.0)
        from_before = jnp.where((here == rows - 1) & (there == 0), 1.0, 0.0)
        lane = iota((8, BLK), 1)
        kind = iota((8, BLK), 0)
        fixes = []
        for face in range(2):
            column = slice(0, BLK) if face == 0 else slice(7 * BLK, 8 * BLK)
            press, vel = stage[0, :, column], stage[2, :, column]
            mixed = 0.5 * (press - vel) if face == 0 else 0.5 * (press + vel)
            pick = jnp.where(lane == (0 if face == 0 else BLK - 1), 1.0, 0.0)
            outgoing = exact_dot(pick, mixed, ((1,), (1,)))[0:1]
            old = aux[face]
            second = (
                exact_dot(old, bend, ((1,), (0,)))
                + exact_dot(aux_sides[0, face], from_after, ((1,), (0,)))
                + exact_dot(aux_sides[1, face], from_before, ((1,), (0,)))
            )
            prior = jnp.concatenate([outgoing, old[:-1]], axis=0)
            new = old + dt * (-rates * old + coupling * (prior - old) + TANGENT * second)
            aux_out[0, face] = new
            incoming = jnp.sum(new, axis=0, keepdims=True) * (1.0 / order)
            ghost_p = outgoing + incoming
            ghost_w = incoming - outgoing if face == 0 else outgoing - incoming
            if face == 0:
                shape = jnp.where(lane == 0, -7.0 / 12.0, 0.0) + jnp.where(lane == 1, 1.0 / 12.0, 0.0)
            else:
                shape = jnp.where(lane == BLK - 1, 7.0 / 12.0, 0.0) + jnp.where(
                    lane == BLK - 2, -1.0 / 12.0, 0.0
                )
            shape = jnp.where(kind == 0, -dt * shape, 0.0)
            wide = [jnp.broadcast_to(g, (8, rows)) for g in (ghost_p, ghost_w)]
            fixes.append([exact_dot(g, shape, ((0,), (0,))) for g in wide])

        def fix(part, which):
            for face, column in ((0, slice(0, BLK)), (1, slice(7 * BLK, 8 * BLK))):
                out[0, part, :, column] = out[0, part, :, column] + fixes[face][which]

        for part in range(1, 4):
            write_part(final, out, part)
        fix(2, 0)
        fix(3, 1)

        for copy in turns:
            copy.wait_send()
        halos.finish()
        count, slots = spread.shape[1:]
        item = iota((1, slots), 1)
        item_turn = lax.shift_right_logical(item * 43691, 19)
        item_rank = item - item_turn * SLOT

        total = jnp.zeros((count, BLK), F32)

        def match(which):
            got = names_in.at[which]
            pltpu.make_async_copy(got, got, name_recv.at[which]).wait()
            listed = names_in[which].reshape(tiles, BLK)
            for part in ((0, 1), (2,))[which]:
                column = jnp.where(iota((BLK, slots), 0) == item_rank + part * LANES, 1.0, 0.0)
                item_name = exact_dot(listed, column, ((1,), (0,)))
                item_name = jnp.where(iota((tiles, slots), 0) == item_turn, item_name, 0.0)
                item_name = jnp.sum(item_name, axis=0, keepdims=True).astype(jnp.int32) - 1
                same = iota((count, slots), 0) == item_name
                spread[part] = jnp.where(same, 1.0, 0.0).astype(BF16)

        def collect(total, which, wave):
            first, end = waves[wave]
            parts = ((0, 1), (2,))[which]
            got = received.at[parts[0] : parts[-1] + 1, first:end]
            pltpu.make_async_copy(got, got, slot_recv.at[which, wave]).wait()
            for part in parts:
                total += jnp.dot(
                    spread[part, :, first * SLOT : end * SLOT],
                    received[part, first:end].reshape((end - first) * SLOT, BLK),
                    preferred_element_type=F32,
                )
            return total

        match(0)
        match(1)
        for wave in range(3):
            total = collect(total, 0, wave)
        for wave in range(3):
            total = collect(total, 1, wave)
        total = collect(total, 0, 3)
        total = collect(total, 1, 3)
        final[0:count, :] = final[0:count, :] + dt * total
        write_part(final, out, 0)
        fix(0, 1)


def store(state, aux, state_out, aux_out, sem):
    copies = [
        pltpu.make_async_copy(a, b, sem.at[i])
        for i, (a, b) in enumerate(((state, state_out), (aux, aux_out)))
    ]
    for copy in copies:
        copy.start()
    for copy in copies:
        copy.wait()


def shards(tiles, fields, face_aux, block_owner):
    _, parts, rows, depth = fields.shape
    order = face_aux.shape[2]
    count = rows * depth // BLK
    span = rows + 2 * HALO
    vmem = pl.BlockSpec(memory_space=pltpu.VMEM)
    hbm = pl.BlockSpec(memory_space=pltpu.HBM)
    dma = pltpu.SemaphoreType.DMA
    fields, face_aux, block_owner = (
        pltpu.with_memory_space_constraint(a, pltpu.HBM) for a in (fields, face_aux, block_owner)
    )
    in_vmem = lambda *arrays: [pltpu.with_memory_space_constraint(a, pltpu.VMEM) for a in arrays]
    stage = pltpu.VMEM((parts, rows, depth), F32)
    wide = pltpu.VMEM((parts * span * 8, BLK), F32)
    exact = pltpu.VMEM((parts * rows * 8, BLK), F32)
    halo = pltpu.VMEM((2, parts * HALO * 8, BLK), BF16)
    slots = (tiles, SLOT // 2, 2, BLK)
    names = (tiles, 1, BLK)
    les, packed, ids = pl.pallas_call(
        functools.partial(les_kernel, tiles),
        out_shape=(
            pltpu.VMEM((parts * rows * 8, BLK), F32), pltpu.VMEM(slots, BF16),
            pltpu.VMEM(names, F32),
        ),
        in_specs=[hbm, hbm],
        out_specs=(vmem, vmem, vmem),
        scratch_shapes=[
            stage, wide, wide, pltpu.VMEM((1, count), jnp.int32), halo, halo,
            pltpu.VMEM((tiles * SLOT, count), BF16), pltpu.VMEM((count, BLK), BF16),
            pltpu.VMEM((2, 8, BLK), F32), dma((3,)), dma, dma((2,)), dma((2,)), dma, dma,
        ],
        compiler_params=pltpu.CompilerParams(
            collective_id=0, has_side_effects=True, vmem_limit_bytes=40 << 20
        ),
    )(fields, block_owner)
    results = pl.pallas_call(
        functools.partial(exchange_kernel, tiles),
        out_shape=(pltpu.VMEM(fields.shape, F32), pltpu.VMEM(face_aux.shape, F32)),
        in_specs=[hbm, hbm, vmem, vmem, vmem],
        out_specs=(vmem, vmem),
        scratch_shapes=[
            stage, wide, exact, pltpu.VMEM((2, order, rows), F32),
            pltpu.VMEM((2, 2, order, rows), F32), halo, halo,
            pltpu.VMEM((2,) + names, F32),
            pltpu.VMEM((3,) + slots, BF16), pltpu.VMEM((3, count, tiles * SLOT), BF16),
            dma((3,)), dma, dma((2,)), dma((2,)), dma((2,)), dma((2,)),
            dma, dma((2,)), dma, dma((2, 4)),
            pltpu.SemaphoreType.REGULAR,
        ],
        compiler_params=pltpu.CompilerParams(
            collective_id=1, has_side_effects=True, vmem_limit_bytes=40 << 20
        ),
    )(fields, face_aux, *in_vmem(les, packed, ids))
    return pl.pallas_call(
        store,
        out_shape=(pltpu.HBM(fields.shape, F32), pltpu.HBM(face_aux.shape, F32)),
        in_specs=[vmem, vmem],
        out_specs=(hbm, hbm),
        scratch_shapes=[dma((2,))],
    )(*in_vmem(*results))


def solution(mesh):
    return jax.shard_map(
        functools.partial(shards, mesh.shape["tile"]),
        mesh=mesh,
        in_specs=(P("grp", None, "tile", None), P("grp", None, None, "tile"), P("grp", "tile")),
        out_specs=(P("grp", None, "tile", None), P("grp", None, None, "tile")),
        check_vma=False,
    )
```

time: 33.4 us -> 27.2 us (0.81)
  the two profiles are of different devices: /device:TPU:1 before, /device:TPU:193 now
where the time goes in v3:
time: 27.2 us; the launch traced here: 27.1 us
  Pallas kernels  26.3 us (97%)
  between operations  0.81 us (3%)
    pallas_call x1, Pallas kernels, shards(): pl.pallas_call(functools.partial(exchange_kernel, tiles), out_shape=(pltp...  25.1 us
    pallas_call x1, Pallas kernels, shards(): pl.pallas_call(store, out_shape=(pltpu.HBM(fields.shape, F32), pltpu.HBM(...  0.99 us

profile of v3, /device:TPU:193, one launch (start us, length us, event | category | flops | bytes accessed | tf_op | source)
XLA Modules:
  0.0 27.1 jit_solution(13486559783597475166)
XLA Ops:
  0.6 0.2 shard_map.50
  0.9 25.1 %shard_map.51 = (f32[1,4,64,1024]{3,2,1,0:T(8,128)S(1)}, f32[1,2,8,64]{3,2,1,0:T(8,128)S(1)}) custom-call(f32[1,4,64,1024]{3,2,1,0:T(8,128)} %fields.3, f32[1,2,8,64]{3,2,1,0:T(8,128)} %face_aux.1, f32[2048,128]{1,0:T(8,128)S(1)} %get-tuple-element.7.les, bf16[64,6,2,128]{3,2,1,0:T(2,128)(2,1)S(1)} %get-tuple-element.8.packed, ...), custom_call_target="tpu_custom_call" | custom-call | tf_op jit(solution)/shard_map/pallas_call | solution.py:608
  26.0 1.0 %shard_map.52 = (f32[1,4,64,1024]{3,2,1,0:T(8,128)}, f32[1,2,8,64]{3,2,1,0:T(8,128)}) custom-call(f32[1,4,64,1024]{3,2,1,0:T(8,128)S(1)} %get-tuple-element.10.state, f32[1,2,8,64]{3,2,1,0:T(8,128)S(1)} %get-tuple-element.11.aux), custom_call_target="tpu_custom_call" | custom-call | tf_op jit(solution)/shard_map/pallas_call | solution.py:626

commit v4 on v3

--- a/solution.py
+++ b/solution.py
@@ -202,7 +202,7 @@
 
 def les_kernel(
     tiles, fields, owner, final, packed, names,
-    stage, state, middle, own, halo_out, halo_in, pack, blocks, ids,
+    stage, state, middle, own, halo_out, halo_in, pack, blocks, inner_slots, ids,
     load_sem, own_sem, halo_send, halo_recv, id_send, id_recv,
 ):
     rows = stage.shape[1]
@@ -254,7 +254,9 @@
             pl.semaphore_wait(barrier, neighbours)
             halos.start()
 
-        pl.when(chip == 3)(meet)
+        early, late = (group < 2) & (chip == 3), (group < 2) & (chip == 0)
+        middling = (group == 2) & ((chip == 0) | (chip == 3))
+        pl.when(early)(meet)
         own_load.wait()
         count = own.shape[1]
         owned = own[...]
@@ -293,10 +295,13 @@
             start = (row - HALO) * 8
             blocks[start : start + size * 8, :] = source_rows(values).reshape(-1, BLK).astype(BF16)
 
+        pl.when((chip == 1) | (chip == 2))(meet)
         first_step(6, rows - 4)
-        pl.when((chip == 1) | (chip == 2))(meet)
+        pl.when(middling)(meet)
         second_step(8, rows - 8)
-        pl.when(chip == 0)(meet)
+        pl.when(late)(meet)
+        inner = slice(count // 4, 3 * count // 4)
+        inner_slots[...] = jnp.dot(pack[:, inner], blocks[inner], preferred_element_type=F32)
         pl.when(paired)(id_copy.start)
         pl.when(paired)(id_copy.wait_recv)
         turns, lane = iota((tiles, BLK), 0), iota((tiles, BLK), 1)
@@ -329,7 +334,9 @@
                 put_rows(final, part, row, values[part], rows)
             start = row * 8
             blocks[start : start + 32, :] = source_rows(values).reshape(-1, BLK).astype(BF16)
-        chosen_blocks = jnp.dot(pack[...], blocks[...], preferred_element_type=F32)
+        chosen_blocks = inner_slots[...]
+        for outer in (slice(0, count // 4), slice(3 * count // 4, count)):
+            chosen_blocks += jnp.dot(pack[:, outer], blocks[outer], preferred_element_type=F32)
         packed[...] = chosen_blocks.astype(BF16).reshape(packed.shape)
         halos.finish()
         pl.when(paired)(id_copy.wait_send)
@@ -350,7 +357,6 @@
     halos = Halos(tiles, tile, state, halo_out, halo_in, halo_send, halo_recv)
     barrier = pltpu.get_barrier_semaphore()
     far = 4 * FAR_COLUMNS
-    waves = [(0, far), (far, far + 24), (far + 24, tiles - 8), (tiles - 8, tiles)]
 
     half = tiles // 2
 
@@ -366,12 +372,11 @@
         for turn in name_turns:
             send_names(turn, which)
         for place, column in enumerate(COLUMNS):
-            wave = sum(end <= 4 * place for _, end in waves)
             for step in order:
                 turn = 4 * place + step
                 pltpu.make_async_remote_copy(
                     packed.at[turn], received.at[group, turn], slot_send,
-                    slot_recv.at[which, wave], device_id=there(column, step), device_id_type=MESH,
+                    slot_recv, device_id=there(column, step), device_id_type=MESH,
                 ).start()
 
     def tell(sem, **there):
@@ -533,37 +538,22 @@
                 same = iota((count, slots), 0) == item_name
                 spread[part] = jnp.where(same, 1.0, 0.0).astype(BF16)
 
-        def collect(total, which, wave):
-            first, end = waves[wave]
-            parts = ((0, 1), (2,))[which]
-            got = received.at[parts[0] : parts[-1] + 1, first:end]
-            pltpu.make_async_copy(got, got, slot_recv.at[which, wave]).wait()
-            for part in parts:
-                total += jnp.dot(
-                    spread[part, :, first * SLOT : end * SLOT],
-                    received[part, first:end].reshape((end - first) * SLOT, BLK),
-                    preferred_element_type=F32,
-                )
-            return total
-
         match(0)
         match(1)
-        for wave in range(3):
-            total = collect(total, 0, wave)
-        for wave in range(3):
-            total = collect(total, 1, wave)
-        total = collect(total, 0, 3)
-        total = collect(total, 1, 3)
+        pltpu.make_async_copy(received, received, slot_recv).wait()
+        for part in range(3):
+            total += jnp.dot(spread[part], received[part].reshape(slots, BLK), preferred_element_type=F32)
         final[0:count, :] = final[0:count, :] + dt * total
         write_part(final, out, 0)
         fix(0, 1)
 
 
 def store(state, aux, state_out, aux_out, sem):
+    parts = state.shape[1]
     copies = [
-        pltpu.make_async_copy(a, b, sem.at[i])
-        for i, (a, b) in enumerate(((state, state_out), (aux, aux_out)))
+        pltpu.make_async_copy(state.at[:, i], state_out.at[:, i], sem.at[i]) for i in range(parts)
     ]
+    copies.append(pltpu.make_async_copy(aux, aux_out, sem.at[parts]))
     for copy in copies:
         copy.start()
     for copy in copies:
@@ -599,7 +589,7 @@
         scratch_shapes=[
             stage, wide, wide, pltpu.VMEM((1, count), jnp.int32), halo, halo,
             pltpu.VMEM((tiles * SLOT, count), BF16), pltpu.VMEM((count, BLK), BF16),
-            pltpu.VMEM((2, 8, BLK), F32), dma((3,)), dma, dma((2,)), dma((2,)), dma, dma,
+            pltpu.VMEM((tiles * SLOT, BLK), F32), pltpu.VMEM((2, 8, BLK), F32), dma((3,)), dma, dma((2,)), dma((2,)), dma, dma,
         ],
         compiler_params=pltpu.CompilerParams(
             collective_id=0, has_side_effects=True, vmem_limit_bytes=40 << 20
@@ -616,7 +606,7 @@
             pltpu.VMEM((2,) + names, F32),
             pltpu.VMEM((3,) + slots, BF16), pltpu.VMEM((3, count, tiles * SLOT), BF16),
             dma((3,)), dma, dma((2,)), dma((2,)), dma((2,)), dma((2,)),
-            dma, dma((2,)), dma, dma((2, 4)),
+            dma, dma((2,)), dma, dma,
             pltpu.SemaphoreType.REGULAR,
         ],
         compiler_params=pltpu.CompilerParams(
@@ -628,7 +618,7 @@
         out_shape=(pltpu.HBM(fields.shape, F32), pltpu.HBM(face_aux.shape, F32)),
         in_specs=[vmem, vmem],
         out_specs=(hbm, hbm),
-        scratch_shapes=[dma((2,))],
+        scratch_shapes=[dma((parts + 1,))],
     )(*in_vmem(*results))
 
 

time: 27.2 us -> 25.1 us (0.923)
  the two profiles are of different devices: /device:TPU:193 before, /device:TPU:1 now
where the time goes in v4:
time: 25.1 us; the launch traced here: 25 us
  Pallas kernels  24.3 us (97%)
  between operations  0.65 us (3%)
    pallas_call x1, Pallas kernels, shards(): pl.pallas_call(functools.partial(exchange_kernel, tiles), out_shape=(pltp...  12.6 us
    pallas_call x1, Pallas kernels, shards(): pl.pallas_call(functools.partial(les_kernel, tiles), out_shape=(pltpu.VME...  10.7 us
    pallas_call x1, Pallas kernels, shards(): pl.pallas_call(store, out_shape=(pltpu.HBM(fields.shape, F32), pltpu.HBM(...  1.01 us

profile of v4, /device:TPU:1, one launch (start us, length us, event | category | flops | bytes accessed | tf_op | source)
XLA Modules:
  0.0 25.0 jit_solution(3679935938537033430)
XLA Ops:
  0.6 10.7 %shard_map.50 = (f32[2048,128]{1,0:T(8,128)S(1)}, bf16[64,6,2,128]{3,2,1,0:T(2,128)(2,1)S(1)}, f32[64,1,128]{2,1,0:T(1,128)S(1)}) custom-call(f32[1,4,64,1024]{3,2,1,0:T(8,128)} %fields.3, s32[1,512]{1,0:T(1,128)} %owner.1), custom_call_target="tpu_custom_call" | custom-call | tf_op jit(solution)/shard_map/pallas_call | solution.py:581
  11.4 12.6 %shard_map.51 = (f32[1,4,64,1024]{3,2,1,0:T(8,128)S(1)}, f32[1,2,8,64]{3,2,1,0:T(8,128)S(1)}) custom-call(f32[1,4,64,1024]{3,2,1,0:T(8,128)} %fields.3, f32[1,2,8,64]{3,2,1,0:T(8,128)} %face_aux.1, f32[2048,128]{1,0:T(8,128)S(1)} %get-tuple-element.7.les, bf16[64,6,2,128]{3,2,1,0:T(2,128)(2,1)S(1)} %get-tuple-element.8.packed, ...), custom_call_target="tpu_custom_call" | custom-call | tf_op jit(solution)/shard_map/pallas_call | solution.py:598
  24.0 1.0 %shard_map.52 = (f32[1,4,64,1024]{3,2,1,0:T(8,128)}, f32[1,2,8,64]{3,2,1,0:T(8,128)}) custom-call(f32[1,4,64,1024]{3,2,1,0:T(8,128)S(1)} %get-tuple-element.10.state, f32[1,2,8,64]{3,2,1,0:T(8,128)S(1)} %get-tuple-element.11.aux), custom_call_target="tpu_custom_call" | custom-call | tf_op jit(solution)/shard_map/pallas_call | solution.py:616

commit v5 on v4

--- a/solution.py
+++ b/solution.py
@@ -21,6 +21,7 @@
 BLK = 128
 SLOT = 12
 LANES = 16
+WIDE = 2 * LANES
 COLUMNS = sorted(range(16), key=lambda c: (-ring(c // 4) - ring(c % 4), c))
 FAR_COLUMNS = sum(ring(c // 4) + ring(c % 4) > 2 for c in COLUMNS)
 HALO = 4
@@ -307,16 +308,16 @@
         turns, lane = iota((tiles, BLK), 0), iota((tiles, BLK), 1)
         chosen_row = jnp.where(iota((tiles, 8), 1) == iota((tiles, 8), 0) // 8, 1.0, 0.0)
         kept = lax.shift_right_logical(lane, 4) == jnp.bitwise_and(turns, 7)
-        folded = jnp.bitwise_and(iota((BLK, BLK), 0), LANES - 1)
+        folded = jnp.bitwise_and(iota((BLK, WIDE), 0), LANES - 1)
 
         def placed(listed, part):
             listed = jnp.where(kept, exact_dot(chosen_row, listed, ((1,), (0,))), 0.0)
-            fold = jnp.where(iota((BLK, BLK), 1) == folded + part * LANES, 1.0, 0.0)
+            fold = jnp.where(iota((BLK, WIDE), 1) == folded + part * LANES, 1.0, 0.0)
             return exact_dot(listed, fold, ((1,), (0,)))
 
         others = jnp.where(paired, ids[1], 0.0)
-        listed = placed(ids[0], group) + placed(others, lax.rem(group + 1, 2))
-        names[...] = listed.reshape(tiles, 1, BLK)
+        listed = placed(ids[0], lax.rem(group, 2)) + placed(others, lax.rem(group + 1, 2))
+        names[...] = listed.reshape(tiles, 1, WIDE)
 
         halos.take()
         tops, bottoms = les_rows(state, 2, 4, span), les_rows(state, rows + 2, 4, span)
@@ -390,7 +391,11 @@
             pl.semaphore_wait(barrier, heard + 1)
             tell(partner_in, grp=1 - mine)
             pl.semaphore_wait(partner_in, 1)
-            send(range(mine * half, (mine + 1) * half), (3, 2, 1, 0))
+            if mine == 0:
+                pl.when(tile == 0)(lambda: pl.semaphore_wait(partner_in, 1))
+            send(range(mine * half, (mine + 1) * half), (2, 1, 3, 0))
+            if mine == 1:
+                pl.when(tile == 0)(lambda: tell(partner_in, grp=0))
             sent = names.at[pl.ds(0, half)]
             pltpu.make_async_copy(sent, sent, name_send).wait()
 
@@ -419,7 +424,10 @@
             for step in range(4):
                 where = tile_at(tile, column, step)
                 tell(barrier, grp=0 if place < FAR_COLUMNS else 1, tile=where)
-                tell(barrier, grp=2, tile=where)
+
+        for place, column in enumerate(COLUMNS):
+            for step in range(4):
+                tell(barrier, grp=2, tile=tile_at(tile, column, step))
 
         loads = row_loads(fields, stage, load_sem)
         aux_load = pltpu.make_async_copy(face_aux.at[0], aux, aux_sem)
@@ -529,9 +537,10 @@
         def match(which):
             got = names_in.at[which]
             pltpu.make_async_copy(got, got, name_recv.at[which]).wait()
-            listed = names_in[which].reshape(tiles, BLK)
+            listed = names_in[which].reshape(tiles, WIDE)
             for part in ((0, 1), (2,))[which]:
-                column = jnp.where(iota((BLK, slots), 0) == item_rank + part * LANES, 1.0, 0.0)
+                lane = item_rank + part % 2 * LANES
+                column = jnp.where(iota((WIDE, slots), 0) == lane, 1.0, 0.0)
                 item_name = exact_dot(listed, column, ((1,), (0,)))
                 item_name = jnp.where(iota((tiles, slots), 0) == item_turn, item_name, 0.0)
                 item_name = jnp.sum(item_name, axis=0, keepdims=True).astype(jnp.int32) - 1
@@ -574,14 +583,14 @@
     in_vmem = lambda *arrays: [pltpu.with_memory_space_constraint(a, pltpu.VMEM) for a in arrays]
     stage = pltpu.VMEM((parts, rows, depth), F32)
     wide = pltpu.VMEM((parts * span * 8, BLK), F32)
-    exact = pltpu.VMEM((parts * rows * 8, BLK), F32)
+    exact = pltpu.VMEM((parts * rows * 8 + 8, BLK), F32)
     halo = pltpu.VMEM((2, parts * HALO * 8, BLK), BF16)
     slots = (tiles, SLOT // 2, 2, BLK)
-    names = (tiles, 1, BLK)
+    names = (tiles, 1, WIDE)
     les, packed, ids = pl.pallas_call(
         functools.partial(les_kernel, tiles),
         out_shape=(
-            pltpu.VMEM((parts * rows * 8, BLK), F32), pltpu.VMEM(slots, BF16),
+            exact, pltpu.VMEM(slots, BF16),
             pltpu.VMEM(names, F32),
         ),
         in_specs=[hbm, hbm],

time: 25.1 us -> 24.9 us (level)
  Pallas kernels: 24.3 us -> 23.9 us
    pallas_call x1, Pallas kernels: 12.6 us -> 12.2 us  [shards(): pl.pallas_call(functools.partial(exchange_kernel, tiles), out_shape=(pltp...]
where the time goes in v5:
time: 24.9 us; the launch traced here: 24.6 us
  Pallas kernels  23.9 us (96%)
  between operations  0.65 us (3%)
    pallas_call x1, Pallas kernels, shards(): pl.pallas_call(functools.partial(exchange_kernel, tiles), out_shape=(pltp...  12.2 us
    pallas_call x1, Pallas kernels, shards(): pl.pallas_call(functools.partial(les_kernel, tiles), out_shape=(exact, pl...  10.7 us
    pallas_call x1, Pallas kernels, shards(): pl.pallas_call(store, out_shape=(pltpu.HBM(fields.shape, F32), pltpu.HBM(...  1.01 us

profile of v5, /device:TPU:1, one launch (start us, length us, event | category | flops | bytes accessed | tf_op | source)
XLA Modules:
  0.0 24.6 jit_solution(2197829530515920954)
XLA Ops:
  0.6 10.7 %shard_map.50 = (f32[2056,128]{1,0:T(8,128)S(1)}, bf16[64,6,2,128]{3,2,1,0:T(2,128)(2,1)S(1)}, f32[64,1,32]{2,1,0:T(1,128)S(1)}) custom-call(f32[1,4,64,1024]{3,2,1,0:T(8,128)} %fields.3, s32[1,512]{1,0:T(1,128)} %owner.1), custom_call_target="tpu_custom_call" | custom-call | tf_op jit(solution)/shard_map/pallas_call | solution.py:590
  11.4 12.2 %shard_map.51 = (f32[1,4,64,1024]{3,2,1,0:T(8,128)S(1)}, f32[1,2,8,64]{3,2,1,0:T(8,128)S(1)}) custom-call(f32[1,4,64,1024]{3,2,1,0:T(8,128)} %fields.3, f32[1,2,8,64]{3,2,1,0:T(8,128)} %face_aux.1, f32[2056,128]{1,0:T(8,128)S(1)} %get-tuple-element.7.les, bf16[64,6,2,128]{3,2,1,0:T(2,128)(2,1)S(1)} %get-tuple-element.8.packed, ...), custom_call_target="tpu_custom_call" | custom-call | tf_op jit(solution)/shard_map/pallas_call | solution.py:607
  23.6 1.0 %shard_map.52 = (f32[1,4,64,1024]{3,2,1,0:T(8,128)}, f32[1,2,8,64]{3,2,1,0:T(8,128)}) custom-call(f32[1,4,64,1024]{3,2,1,0:T(8,128)S(1)} %get-tuple-element.10.state, f32[1,2,8,64]{3,2,1,0:T(8,128)S(1)} %get-tuple-element.11.aux), custom_call_target="tpu_custom_call" | custom-call | tf_op jit(solution)/shard_map/pallas_call | solution.py:625

commit v6 on v5

--- a/solution.py
+++ b/solution.py
@@ -372,13 +372,15 @@
         which = 1 if len(name_turns) == tiles else 0
         for turn in name_turns:
             send_names(turn, which)
-        for place, column in enumerate(COLUMNS):
-            for step in order:
-                turn = 4 * place + step
-                pltpu.make_async_remote_copy(
-                    packed.at[turn], received.at[group, turn], slot_send,
-                    slot_recv, device_id=there(column, step), device_id_type=MESH,
-                ).start()
+        split = 11
+        turns = [4 * place + step for place in range(split) for step in order]
+        for part in (order[:2], order[2:]):
+            turns += [4 * place + step for place in range(split, 16) for step in part]
+        for turn in turns:
+            pltpu.make_async_remote_copy(
+                packed.at[turn], received.at[group, turn], slot_send, slot_recv,
+                device_id=there(COLUMNS[turn // 4], turn % 4), device_id_type=MESH,
+            ).start()
 
     def tell(sem, **there):
         pl.semaphore_signal(sem, inc=1, device_id=there, device_id_type=MESH)

time: 24.9 us -> 24.9 us (level)
  no operation moved by 1% of the time
where the time goes in v6:
time: 24.9 us; the launch traced here: 24.6 us
  Pallas kernels  23.9 us (96%)
  between operations  0.65 us (3%)
    pallas_call x1, Pallas kernels, shards(): pl.pallas_call(functools.partial(exchange_kernel, tiles), out_shape=(pltp...  12.2 us
    pallas_call x1, Pallas kernels, shards(): pl.pallas_call(functools.partial(les_kernel, tiles), out_shape=(exact, pl...  10.7 us
    pallas_call x1, Pallas kernels, shards(): pl.pallas_call(store, out_shape=(pltpu.HBM(fields.shape, F32), pltpu.HBM(...  1.01 us

profile of v6, /device:TPU:1, one launch (start us, length us, event | category | flops | bytes accessed | tf_op | source)
XLA Modules:
  0.0 24.6 jit_solution(14746008280582112606)
XLA Ops:
  0.6 10.7 %shard_map.50 = (f32[2056,128]{1,0:T(8,128)S(1)}, bf16[64,6,2,128]{3,2,1,0:T(2,128)(2,1)S(1)}, f32[64,1,32]{2,1,0:T(1,128)S(1)}) custom-call(f32[1,4,64,1024]{3,2,1,0:T(8,128)} %fields.3, s32[1,512]{1,0:T(1,128)} %owner.1), custom_call_target="tpu_custom_call" | custom-call | tf_op jit(solution)/shard_map/pallas_call | solution.py:592
  11.4 12.2 %shard_map.51 = (f32[1,4,64,1024]{3,2,1,0:T(8,128)S(1)}, f32[1,2,8,64]{3,2,1,0:T(8,128)S(1)}) custom-call(f32[1,4,64,1024]{3,2,1,0:T(8,128)} %fields.3, f32[1,2,8,64]{3,2,1,0:T(8,128)} %face_aux.1, f32[2056,128]{1,0:T(8,128)S(1)} %get-tuple-element.7.les, bf16[64,6,2,128]{3,2,1,0:T(2,128)(2,1)S(1)} %get-tuple-element.8.packed, ...), custom_call_target="tpu_custom_call" | custom-call | tf_op jit(solution)/shard_map/pallas_call | solution.py:609
  23.6 1.0 %shard_map.52 = (f32[1,4,64,1024]{3,2,1,0:T(8,128)}, f32[1,2,8,64]{3,2,1,0:T(8,128)}) custom-call(f32[1,4,64,1024]{3,2,1,0:T(8,128)S(1)} %get-tuple-element.10.state, f32[1,2,8,64]{3,2,1,0:T(8,128)S(1)} %get-tuple-element.11.aux), custom_call_target="tpu_custom_call" | custom-call | tf_op jit(solution)/shard_map/pallas_call | solution.py:627
